TPU v7x, 256 devices: a whole 4x4x8 slice. The times are simulated.
256 devices in a mesh: tm: 8 (over x, core), pair: 32 (over y, z).
Axes of the slice: x: 4, y: 4, z: 8, core: 2. Of those that a mesh axis runs over, the one named last changes fastest.
Arguments:
- coefs: bfloat16 [2048, 256, 2048], P('pair', None, 'tm'), may hold values from -0.8919053 to 0.8919053
- energies: bfloat16 [2048, 2048], P('pair', 'tm'), may hold values from 0.0195 to 16
- coulomb: bfloat16 [32, 32, 256, 256], P('pair', 'tm'), may hold values from -0.375 to 0.375
- tau_grid: float32 [3], replicated, may hold values from 0.0079 to 5.01
- freq_grid: float32 [3], replicated, may hold values from 0.2 to 5
- pairs: int32 [32, 32, 2], replicated, may hold values from -1 to 2047, as said below
Outputs:
- screened: bfloat16 [32, 32, 3, 256, 256], P('pair', 'tm')
- self_energy: float32 [2048, 2048], P('pair', 'tm')
Inputs may be any that keep to these rules, and one draw needn't show every extreme that they name: Entry 0 of pairs[d,k] is a global block or -1, entry 1 a block index below 64 of device d, -1 exactly where entry 0 is -1. Padding forms the tail of each row and some row has none. No row names more than 2 blocks held by one index of pair, and some row names exactly 2.
All inputs are finite; a program needn't handle non-finite values.
Results may differ from a plain program's by a relative error of at most 0.02.
Values may be sent and summed in bfloat16 or wider, within the bound.
A program may use at most 128 MiB of HBM per device.

v0:
```python
import math

import jax
import jax.numpy as jnp
from jax import lax
from jax.sharding import PartitionSpec as P

SLOTS = 64


def dress(coef_block, expo, tvalue):
    decay = jnp.exp(-tvalue * expo.astype(jnp.float32))
    return (coef_block.astype(jnp.float32) * decay[:, None, :]).astype(jnp.bfloat16)


def screen_tiles(chi, tile, tau_grid, freq_grid, aux_count, time_count):
    hi = lax.Precision.HIGHEST
    cosine = jnp.cos(freq_grid[:, None] * tau_grid[None, :])
    chiw = jnp.einsum("wt,ktpq->kwpq", cosine, chi, precision=hi).astype(jnp.bfloat16)
    prod = jnp.einsum("kwpq,kqr->kwpr", chiw, tile, preferred_element_type=jnp.float32)
    prod_b = prod.astype(jnp.bfloat16)
    wfreq = prod + jnp.einsum(
        "kwpq,kwqr->kwpr", prod_b, prod_b, preferred_element_type=jnp.float32
    ) / math.sqrt(aux_count)
    return (jnp.einsum("wt,kwpq->ktpq", cosine, wfreq, precision=hi) / time_count).astype(
        jnp.bfloat16
    )


def body(coefs, energies, coulomb, tau_grid, freq_grid, pairs):
    blocks, aux_count, slice_len = coefs.shape
    pair_count = lax.axis_size("pair")
    time_count = tau_grid.shape[0]
    listed = pairs.shape[1]
    capacity = SLOTS // pair_count
    my_pair = lax.axis_index("pair")
    hi = lax.Precision.HIGHEST
    remote_all = pairs[:, :, 0]
    live_all = remote_all >= 0
    source_all = jnp.where(live_all, remote_all // blocks, -1)
    mine = live_all & (source_all == my_pair)
    rank = jnp.cumsum(mine.astype(jnp.int32), axis=1) - 1
    slot_ids = jnp.arange(capacity, dtype=jnp.int32)
    slot_hit = mine[:, None, :] & (rank[:, None, :] == slot_ids[None, :, None])
    held_idx = jnp.where(live_all, remote_all % blocks, 0)
    picked = jnp.sum(jnp.where(slot_hit, held_idx[:, None, :], 0), axis=2).reshape(-1)
    valid = jnp.any(slot_hit, axis=2).reshape(-1)
    send_keep = valid.astype(jnp.bfloat16)
    send_coef = coefs[picked] * send_keep[:, None, None]
    send_ener = energies[picked] * send_keep[:, None]
    recv_coef, recv_ener = (
        lax.all_to_all(send_coef, "pair", split_axis=0, concat_axis=0, tiled=True),
        lax.all_to_all(send_ener, "pair", split_axis=0, concat_axis=0, tiled=True),
    )
    own_row = lax.dynamic_index_in_dim(pairs, my_pair, 0, keepdims=False)
    remote = own_row[:, 0]
    local = own_row[:, 1]
    alive = remote >= 0
    source = jnp.where(alive, remote // blocks, 0)
    positions = jnp.arange(listed, dtype=jnp.int32)
    earlier = (
        (source[:, None] == source[None, :])
        & alive[None, :]
        & (positions[None, :] < positions[:, None])
    )
    slot_of = jnp.sum(earlier.astype(jnp.int32), axis=1)
    buffer_idx = jnp.where(alive, source * capacity + slot_of, 0)
    keep = alive.astype(jnp.bfloat16)
    coef_g = recv_coef[buffer_idx] * keep[:, None, None]
    ener_g = recv_ener[buffer_idx]
    local_idx = jnp.where(alive, local, 0)
    coef_a = coefs[local_idx] * keep[:, None, None]
    ener_a = energies[local_idx]
    dressed_a = []
    dressed_g = []
    partial_list = []
    for tpoint in range(time_count):
        xa = dress(coef_a, ener_a, tau_grid[tpoint])
        yg = dress(coef_g, ener_g, tau_grid[tpoint])
        dressed_a.append(xa)
        dressed_g.append(yg)
        partial_list.append(jnp.einsum("kpm,kqm->kpq", xa, yg, preferred_element_type=jnp.float32))
    partial_value = jnp.stack(partial_list, axis=1)
    chi = lax.psum_scatter(
        partial_value.astype(jnp.bfloat16), "tm", scatter_dimension=0, tiled=True
    ).astype(jnp.float32)
    wtime = screen_tiles(chi, coulomb[0], tau_grid, freq_grid, aux_count, time_count)
    stacked_a = jnp.stack(dressed_a, axis=0)
    stacked_g = jnp.stack(dressed_g, axis=0)
    piece = lax.all_gather(wtime, "tm", axis=0, tiled=True)
    count = piece.shape[0]
    total = jnp.zeros((count, stacked_a.shape[3]), jnp.float32)
    for tpoint in range(time_count):
        applied = jnp.einsum(
            "kpq,kqm->kpm", piece[:, tpoint], stacked_g[tpoint], preferred_element_type=jnp.float32
        )
        total = total + jnp.sum(stacked_a[tpoint].astype(jnp.float32) * applied, axis=1)
    contrib = total / time_count
    flat_slots = jnp.arange(pair_count * capacity, dtype=jnp.int32)
    placing = ((flat_slots[:, None] == buffer_idx[None, :]) & alive[None, :]).astype(jnp.float32)
    outgoing = jnp.dot(placing, contrib, precision=hi, preferred_element_type=jnp.float32)
    incoming = lax.all_to_all(outgoing, "pair", split_axis=0, concat_axis=0, tiled=True)
    block_ids = jnp.arange(blocks, dtype=jnp.int32)
    owning = ((block_ids[:, None] == picked[None, :]) & valid[None, :]).astype(jnp.float32)
    self_energy = jnp.dot(owning, incoming, precision=hi, preferred_element_type=jnp.float32)
    return (wtime[None], self_energy)


def solution(mesh):
    return jax.shard_map(
        body,
        mesh=mesh,
        in_specs=(
            P("pair", None, "tm"),
            P("pair", "tm"),
            P("pair", "tm", None, None),
            P(),
            P(),
            P(),
        ),
        out_specs=(P("pair", "tm", None, None, None), P("pair", "tm")),
        check_vma=False,
    )
```

profile of v0, /device:TPU:1, one launch (start us, length us, event | category | flops | bytes accessed | tf_op | source)
XLA Modules:
  0.0 544.6 jit_solution(838076935627180041)
XLA Ops:
  7.2 0.8 slice.33
  8.0 0.2 reduce_window_sum.11
  8.2 0.1 fusion.62
  8.4 0.1 select_reduce_fusion
  8.5 0.1 copy.27
  8.6 0.1 copy.25
  8.7 0.1 reshape.250
  8.8 1.4 gather_fusion.4
  10.3 0.7 broadcast_multiply_fusion.3
  11.0 12.0 %all-to-all-start.1 = ((bf16[32,2,256]{2,1,0:T(2,128)(2,1)}), bf16[32,2,256]{2,1,0:T(2,128)(2,1)S(1)}, u32[]{:S(2)}, u32[]{:S(2)}) async-start(bf16[32,2,256]{2,1,0:T(2,128)(2,1)} %broadcast_multiply_fusion.3), calls=%async_computation.1 | async-start | bytes 65536 | tf_op jit(solution)/shard_map/all_to_all | solution.py:53
  23.0 0.1 copy.26
  23.1 0.1 reshape.251
  23.3 8.8 %gather_fusion.2 = bf16[64,256,256]{2,1,0:T(8,128)(2,1)} fusion(bf16[64,256,256]{2,1,0:T(8,128)(2,1)} %param.6, s32[1024]{0:T(1024)S(1)} %pad_clamp_fusion.1), kind=kCustom, calls=%fused_computation.2 | custom fusion | bytes 16777472 | tf_op jit(solution)/shard_map/gather | solution.py:49
  32.0 7.2 %broadcast_multiply_fusion = bf16[64,256,256]{2,1,0:T(8,128)(2,1)} fusion(bf16[64,256,256]{2,1,0:T(8,128)(2,1)} %gather_fusion.2, bf16[64]{0:T(256)(128)(2,1)S(1)} %convert_element_type.121), kind=kLoop, calls=%fused_computation.34 | loop fusion | flops 4194304 | bytes 16777344 | tf_op jit(solution)/shard_map/mul | solution.py:49
  39.2 9.5 %all-to-all-start = ((bf16[64,256,256]{2,1,0:T(8,128)(2,1)}), bf16[64,256,256]{2,1,0:T(8,128)(2,1)}, u32[]{:S(2)}, u32[]{:S(2)}) async-start(bf16[64,256,256]{2,1,0:T(8,128)(2,1)} %broadcast_multiply_fusion), calls=%async_computation | async-start | bytes 16777216 | tf_op jit(solution)/shard_map/all_to_all | solution.py:52
  48.8 0.7 dynamic-slice_bitcast_fusion
  49.5 0.6 gather_fusion.1
  50.1 6.1 %gather_fusion = bf16[32,256,256]{2,1,0:T(8,128)(2,1)} fusion(bf16[64,256,256]{2,1,0:T(8,128)(2,1)} %param.6, s32[1024]{0:T(1024)S(1)} %pad_clamp_fusion.2), kind=kCustom, calls=%fused_computation | custom fusion | bytes 8388736 | tf_op jit(solution)/shard_map/gather | solution.py:72
  56.3 0.6 fusion.96
  58.8 0.2 convert_reduce_fusion
  59.1 0.6 gather_fusion.5
  59.8 172.3 %all-to-all-done = bf16[64,256,256]{2,1,0:T(8,128)(2,1)} async-done(((bf16[64,256,256]{2,1,0:T(8,128)(2,1)}), bf16[64,256,256]{2,1,0:T(8,128)(2,1)}, u32[]{:S(2)}, u32[]{:S(2)}) %all-to-all-start) | async-done | bytes 8388640 | tf_op jit(solution)/shard_map/all_to_all | solution.py:52
  232.0 6.1 %gather_fusion.3 = bf16[32,256,256]{2,1,0:T(8,128)(2,1)} fusion(bf16[64,256,256]{2,1,0:T(8,128)(2,1)} %all-to-all-done, s32[1024]{0:T(1024)S(1)} %pad_clamp_fusion), kind=kCustom, calls=%fused_computation.3 | custom fusion | bytes 8388736 | tf_op jit(solution)/shard_map/gather | solution.py:69
  238.2 5.9 %convert_bitcast_fusion = bf16[32,1,256,256]{3,2,0,1:T(8,128)(2,1)S(1)} fusion(f32[32,256]{1,0:T(8,128)S(1)} %get-tuple-element.17, f32[32,256]{1,0:T(8,128)S(1)} %get-tuple-element.14, bf16[32,256,256]{2,1,0:T(8,128)(2,1)} %gather_fusion, bf16[32]{0:T(256)(128)(2,1)S(1)} %get-tuple-element.18, bf16[32,256,256]{2,1,0:T(8,128)(2,1)} %gather_fusion.3), kind=kOutput, calls=%fused_computation.31 | convolution fusion | flops 1092616192 | bytes 12648512 | tf_op jit(solution)/shard_map/kpm,kqm->kpq/dot_general | solution.py:82
  244.1 2.5 convert_bitcast_fusion.1
  246.6 3.9 convert_bitcast_fusion.2
  250.5 7.9 %pad_maximum_fusion = bf16[32,3,256,256]{3,2,0,1:T(8,128)(2,1)} fusion(bf16[32,1,256,256]{3,2,0,1:T(8,128)(2,1)S(1)} %convert_bitcast_fusion, bf16[32,1,256,256]{3,2,0,1:T(8,128)(2,1)S(1)} %convert_bitcast_fusion.1, bf16[32,1,256,256]{3,2,0,1:T(8,128)(2,1)} %convert_bitcast_fusion.2), kind=kLoop, calls=%fused_computation.6 | loop fusion | flops 12582912 | bytes 25165824 | tf_op jit(solution)/shard_map/stack | solution.py:83
  258.4 0.2 all-gather.2.cloned.1.call-start
  258.6 0.4 copy-done.8
  259.0 0.6 dynamic-slice
  260.3 151.5 %all-reduce.3.cloned.1.call-done = bf16[32,3,256,256]{3,2,0,1:T(8,128)(2,1)} async-done(((bf16[32,3,256,256]{3,2,0,1:T(8,128)(2,1)}), bf16[32,3,256,256]{3,2,0,1:T(8,128)(2,1)}) %all-reduce.3.cloned.1.call-update) | async-done | bytes 12582928
  411.7 1.5 constant_dynamic-slice_fusion
  413.3 4.1 convert_bitcast_fusion.3
  417.4 0.6 fusion.47
  417.9 0.6 multiply_add_fusion
  418.5 9.5 %multiply_convert_fusion = bf16[4,256,256,3]{2,3,1,0:T(4,128)(2,1)S(1)} fusion(f32[4,3,256,256]{3,2,1,0:T(8,128)S(1)} %multiply_add_fusion, f32[3]{0:T(128)S(1)} %copy-done.6, f32[3]{0:T(128)S(1)} %copy-done.7), kind=kOutput, calls=%fused_computation.30 | convolution fusion | flops 29884424 | bytes 4718616 | tf_op jit(solution)/shard_map/wt,kwpq->ktpq/dot_general | solution.py:25
  428.0 1.4 copy.33
  429.5 70.6 %all-gather.2.cloned.1.call-done = bf16[32,3,256,256]{3,2,1,0:T(8,128)(2,1)} async-done(((bf16[4,3,256,256]{3,2,1,0:T(8,128)(2,1)}), bf16[32,3,256,256]{3,2,1,0:T(8,128)(2,1)}) %all-gather.2.cloned.1.call-update) | async-done | bytes 12582928 | tf_op jit(solution)/shard_map/all_gather | solution.py:90
  500.1 7.5 %multiply_reduce_fusion.1 = f32[32,256]{1,0:T(8,128)S(1)} fusion(f32[32,256]{1,0:T(8,128)S(1)} %get-tuple-element.13, f32[32,256]{1,0:T(8,128)S(1)} %get-tuple-element.16, bf16[32,3,256,256]{3,2,1,0:T(8,128)(2,1)} %all-gather.2.cloned.1.call-done, bf16[32,256,256]{2,1,0:T(8,128)(2,1)} %gather_fusion, bf16[32]{0:T(256)(128)(2,1)S(1)} %get-tuple-element.18, ...), kind=kOutput, calls=%fused_computation.20 | convolution fusion | flops 1096802304 | bytes 12682240 | tf_op jit(solution)/shard_map/kpq,kqm->kpm/dot_general | solution.py:94
  507.6 5.0 multiply_reduce_fusion.2
  512.6 5.0 multiply_reduce_fusion
  517.6 0.2 fusion.57
  517.8 0.7 all_to_all.20
  518.5 9.6 %all-to-all-start.2 = ((f32[32,2,256]{2,1,0:T(2,128)}), f32[32,2,256]{2,1,0:T(2,128)S(1)}, u32[]{:S(2)}, u32[]{:S(2)}) async-start(f32[32,2,256]{2,1,0:T(2,128)} %all_to_all.20), calls=%async_computation.2 | async-start | bytes 131072 | tf_op jit(solution)/shard_map/all_to_all | solution.py:102
  528.0 0.1 eq.82
  528.1 1.4 copy.37
  529.5 7.4 %all-to-all-done.2 = f32[32,2,256]{2,1,0:T(2,128)S(1)} async-done(((f32[32,2,256]{2,1,0:T(2,128)}), f32[32,2,256]{2,1,0:T(2,128)S(1)}, u32[]{:S(2)}, u32[]{:S(2)}) %all-to-all-start.2) | async-done | bytes 65568 | tf_op jit(solution)/shard_map/all_to_all | solution.py:102
  537.0 0.8 fusion.64
  (39 shorter events, 0.4 us)
Async XLA Ops:
  7.2 410.2 %copy-start = (bf16[1,4,256,256]{3,2,1,0:T(8,128)(2,1)S(1)}, bf16[1,4,256,256]{3,2,1,0:T(8,128)(2,1)}, u32[]{:S(2)}) copy-start(bf16[1,4,256,256]{3,2,1,0:T(8,128)(2,1)} %param.8) | copy-start | bytes 1572868
  11.0 28.2 %all-to-all-start.1 = ((bf16[32,2,256]{2,1,0:T(2,128)(2,1)}), bf16[32,2,256]{2,1,0:T(2,128)(2,1)S(1)}, u32[]{:S(2)}, u32[]{:S(2)}) async-start(bf16[32,2,256]{2,1,0:T(2,128)(2,1)} %broadcast_multiply_fusion.3), calls=%async_computation.1 | async-start | bytes 65536 | tf_op jit(solution)/shard_map/all_to_all | solution.py:53
  39.2 10.3 %copy-start.1 = (bf16[64,256]{1,0:T(8,128)(2,1)S(1)}, bf16[64,256]{1,0:T(8,128)(2,1)}, u32[]{:S(2)}) copy-start(bf16[64,256]{1,0:T(8,128)(2,1)} %param.7) | copy-start | bytes 98308
  39.2 192.8 %all-to-all-start = ((bf16[64,256,256]{2,1,0:T(8,128)(2,1)}), bf16[64,256,256]{2,1,0:T(8,128)(2,1)}, u32[]{:S(2)}, u32[]{:S(2)}) async-start(bf16[64,256,256]{2,1,0:T(8,128)(2,1)} %broadcast_multiply_fusion), calls=%async_computation | async-start | bytes 16777216 | tf_op jit(solution)/shard_map/all_to_all | solution.py:52
  48.7 363.0 %all-reduce.3.cloned.1.call-start = ((), (), s32[]{:S(2)}) async-start(), calls=%async_computation.4 | async-start | bytes 25165824
  50.1 6.2 %copy-start.6 = (f32[3]{0:T(128)S(1)}, f32[3]{0:T(128)}, u32[]{:S(2)}) copy-start(f32[3]{0:T(128)} %param.9) | copy-start | bytes 40
  238.2 5.9 %copy-start.2 = (bf16[32,256,256]{2,1,0:T(8,128)(2,1)S(1)}, bf16[32,256,256]{2,1,0:T(8,128)(2,1)}, u32[]{:S(2)}) copy-start(bf16[32,256,256]{2,1,0:T(8,128)(2,1)} %gather_fusion) | copy-start | bytes 12582916
  238.2 5.9 %copy-start.4 = (bf16[32,256,256]{2,1,0:T(8,128)(2,1)S(1)}, bf16[32,256,256]{2,1,0:T(8,128)(2,1)}, u32[]{:S(2)}) copy-start(bf16[32,256,256]{2,1,0:T(8,128)(2,1)} %gather_fusion.3) | copy-start | bytes 12582916
  258.4 0.7 copy-start.8
  258.4 154.9 %copy-start.7 = (f32[3]{0:T(128)S(1)}, f32[3]{0:T(128)}, u32[]{:S(2)}) copy-start(f32[3]{0:T(128)} %param.10) | copy-start | bytes 40
  258.4 241.7 %all-gather.2.cloned.1.call-start = ((), (), s32[]{:S(2)}) async-start(), calls=%async_computation.3 | async-start | bytes 14155776 | tf_op jit(solution)/shard_map/all_gather | solution.py:90
  500.1 7.5 %copy-start.3 = (bf16[32,256,256]{2,1,0:T(8,128)(2,1)S(1)}, bf16[32,256,256]{2,1,0:T(8,128)(2,1)}, u32[]{:S(2)}) copy-start(bf16[32,256,256]{2,1,0:T(8,128)(2,1)} %gather_fusion) | copy-start | bytes 12582916
  500.1 7.5 %copy-start.5 = (bf16[32,256,256]{2,1,0:T(8,128)(2,1)S(1)}, bf16[32,256,256]{2,1,0:T(8,128)(2,1)}, u32[]{:S(2)}) copy-start(bf16[32,256,256]{2,1,0:T(8,128)(2,1)} %gather_fusion.3) | copy-start | bytes 12582916
  518.5 18.5 %all-to-all-start.2 = ((f32[32,2,256]{2,1,0:T(2,128)}), f32[32,2,256]{2,1,0:T(2,128)S(1)}, u32[]{:S(2)}, u32[]{:S(2)}) async-start(f32[32,2,256]{2,1,0:T(2,128)} %all_to_all.20), calls=%async_computation.2 | async-start | bytes 131072 | tf_op jit(solution)/shard_map/all_to_all | solution.py:102
Sparse Core Ops, SparseCore 0:
  258.5 153.1 all-reduce.2
  429.6 70.4 all-gather.1
where the time goes:
time: 546 us; the launch traced here: 545 us
  waiting for transfers between devices  402 us (74%)
  matrix products  45.4 us (8%)
  local copies, waits for them, and re-layouts  32.6 us (6%)
  starting transfers between devices  31.4 us (6%)
  between operations  16.9 us (3%)
  other arithmetic  16.6 us (3%)
    all_to_all x1, waiting for transfers between devices, body(): lax.all_to_all(send_coef, 'pair', split_axis=0, concat_axis=0, tiled=True)  172 us
    unnamed x3, waiting for transfers between devices  151 us
    all_gather x1, waiting for transfers between devices, body(): piece = lax.all_gather(wtime, 'tm', axis=0, tiled=True)  70.6 us
    dot_general x3, matrix products, body(): jnp.einsum('kpq,kqm->kpm', piece[:, tpoint], stacked_g[tpoint], preferred...  17.5 us
    dot_general x3, matrix products, body(): jnp.einsum('kpm,kqm->kpq', xa, yg, preferred_element_type=jnp.float32)  12.3 us
    all_to_all x1, starting transfers between devices, body(): lax.all_to_all(send_ener, 'pair', split_axis=0, concat_axis=0, tiled=True)  12 us
  transfers between devices with their start and end apart: 5, of which 4 were waited for; matrix products, arithmetic and copies ran while one was open for 5% of the time, Pallas kernels for 0%

commit v1 on v0

v1 whole, which is shorter than its diff:
```python
import functools
import math

import jax
import jax.numpy as jnp
from jax import lax
from jax.experimental import pallas as pl
from jax.experimental.pallas import tpu as pltpu
from jax.sharding import PartitionSpec as P

CAP = 2
CHUNKS = 4
MESH = pl.DeviceIdType.MESH


def greet(n_tm, n_pair, my_tm, my_pair):
    barrier = pltpu.get_barrier_semaphore()

    def pair_peer(i, c):
        other = lax.rem(my_pair + i, n_pair)
        pl.semaphore_signal(barrier, inc=1, device_id=(my_tm, other), device_id_type=MESH)
        return c

    def tm_peer(i, c):
        other = lax.rem(my_tm + i, n_tm)
        pl.semaphore_signal(barrier, inc=1, device_id=(other, my_pair), device_id_type=MESH)
        return c

    lax.fori_loop(1, n_pair, pair_peer, 0)
    lax.fori_loop(1, n_tm, tm_peer, 0)
    pl.semaphore_wait(barrier, n_pair + n_tm - 2)


def wait_bytes(ref, sem):
    pltpu.make_async_copy(ref, ref, sem).wait()


def gather_kernel(
    n_tm, n_pair, own, rows,
    slot_ref, local_ref, pick_ref, coef_ref, ener_ref,
    a_out, g_out, e_out,
    *scratch,
):
    my_tm, my_pair = lax.axis_index("tm"), lax.axis_index("pair")
    sends, recvs = scratch[:CHUNKS], scratch[CHUNKS : 2 * CHUNKS]
    (e_send, e_recv, a_send, g_send, x_ener,
     pair_send, pair_recv, a_sems, g_sems, e_sems, own_sems) = scratch[2 * CHUNKS :]
    peers, others = n_pair - 1, n_tm - 1
    step = rows // CHUNKS
    greet(n_tm, n_pair, my_tm, my_pair)

    def pair_copy(i, c):
        target = lax.rem(my_pair + i + 1, n_pair)
        return pltpu.make_async_remote_copy(
            src_ref=sends[c].at[pl.ds(CAP * i, CAP)],
            dst_ref=recvs[c].at[pl.ds(CAP * i, CAP)],
            send_sem=pair_send.at[c], recv_sem=pair_recv.at[c],
            device_id=(my_tm, target), device_id_type=MESH,
        )

    def ener_copy(i):
        target = lax.rem(my_pair + i + 1, n_pair)
        return pltpu.make_async_remote_copy(
            src_ref=e_send.at[i], dst_ref=e_recv.at[i],
            send_sem=pair_send.at[CHUNKS], recv_sem=pair_recv.at[CHUNKS],
            device_id=(my_tm, target), device_id_type=MESH,
        )

    row_id = lax.broadcasted_iota(jnp.int32, (16, ener_ref.shape[2]), 0)

    def stage_a(u):
        owner = lax.rem(my_tm + u + 1, n_tm)
        for e in range(own):
            a_send[u, e] = coef_ref[local_ref[owner * own + e]]
        return owner

    def send_pair(c):
        def one(i, carry):
            for j in range(CAP):
                sends[c][CAP * i + j] = coef_ref[pick_ref[CAP * i + j], pl.ds(c * step, step), :]
            pair_copy(i, c).start()
            return carry

        lax.fori_loop(0, peers, one, 0)
        for j in range(CAP):
            recvs[c][CAP * peers + j] = coef_ref[pick_ref[CAP * peers + j], pl.ds(c * step, step), :]

    def stage_ener(i):
        tile = jnp.zeros(row_id.shape, jnp.float32)
        for j in range(CAP):
            tile = jnp.where(row_id == j, ener_ref[pick_ref[CAP * i + j]].astype(jnp.float32), tile)
        return tile.astype(jnp.bfloat16)

    def send_ener(i, carry):
        e_send[i] = stage_ener(i)
        ener_copy(i).start()
        return carry

    def a_one(u, carry):
        owner = stage_a(u)
        pltpu.make_async_remote_copy(
            src_ref=a_send.at[u], dst_ref=a_out.at[my_tm],
            send_sem=a_sems.at[0], recv_sem=a_sems.at[1],
            device_id=(owner, my_pair), device_id_type=MESH,
        ).start()
        return carry

    send_pair(0)
    lax.fori_loop(0, others, a_one, 0)
    stage_a(others)
    own_a = pltpu.make_async_copy(a_send.at[others], a_out.at[my_tm], own_sems.at[0])
    own_a.start()
    lax.fori_loop(0, peers, send_ener, 0)
    e_recv[peers] = stage_ener(peers)
    for c in range(1, CHUNKS):
        send_pair(c)

    owned_g = []
    for c in range(CHUNKS):
        wait_bytes(recvs[c].at[pl.ds(0, CAP * peers)], pair_recv.at[c])

        def stage_g(u):
            owner = lax.rem(my_tm + u + 1, n_tm)
            for e in range(own):
                g_send[c, u, e] = recvs[c][slot_ref[owner * own + e]]
            return owner

        def g_one(u, carry):
            owner = stage_g(u)
            pltpu.make_async_remote_copy(
                src_ref=g_send.at[c, u], dst_ref=g_out.at[c, my_tm],
                send_sem=g_sems.at[0, c], recv_sem=g_sems.at[1, c],
                device_id=(owner, my_pair), device_id_type=MESH,
            ).start()
            return carry

        lax.fori_loop(0, others, g_one, 0)
        stage_g(others)
        copy = pltpu.make_async_copy(g_send.at[c, others], g_out.at[c, my_tm], own_sems.at[1 + c])
        copy.start()
        owned_g.append(copy)
        if c == 0:
            wait_bytes(e_recv.at[pl.ds(0, peers)], pair_recv.at[CHUNKS])

            def stage_x(u):
                owner = lax.rem(my_tm + u + 1, n_tm)
                tile = jnp.zeros(row_id.shape, jnp.float32)
                for e in range(own):
                    slot = slot_ref[owner * own + e]
                    held = e_recv[slot // CAP].astype(jnp.float32)
                    picked = jnp.sum(jnp.where(row_id == lax.rem(slot, CAP), held, 0.0), axis=0, keepdims=True)
                    tile = jnp.where(row_id == e, picked, tile)
                    mine = ener_ref[local_ref[owner * own + e]].astype(jnp.float32)
                    tile = jnp.where(row_id == own + e, mine, tile)
                x_ener[u] = tile.astype(jnp.bfloat16)
                return owner

            def x_one(u, carry):
                owner = stage_x(u)
                pltpu.make_async_remote_copy(
                    src_ref=x_ener.at[u], dst_ref=e_out.at[my_tm],
                    send_sem=e_sems.at[0], recv_sem=e_sems.at[1],
                    device_id=(owner, my_pair), device_id_type=MESH,
                ).start()
                return carry

            lax.fori_loop(0, others, x_one, 0)
            stage_x(others)
            own_e = pltpu.make_async_copy(x_ener.at[others], e_out.at[my_tm], own_sems.at[1 + CHUNKS])
            own_e.start()

    for c in range(CHUNKS):
        wait_bytes(sends[c].at[pl.ds(0, CAP * peers)], pair_send.at[c])
    wait_bytes(e_send.at[pl.ds(0, peers)], pair_send.at[CHUNKS])
    for side in range(2):
        wait_bytes(a_send.at[pl.ds(0, others)], a_sems.at[side])
        wait_bytes(x_ener.at[pl.ds(0, others)], e_sems.at[side])
        for c in range(CHUNKS):
            wait_bytes(g_send.at[c, pl.ds(0, others)], g_sems.at[side, c])
    own_a.wait()
    own_e.wait()
    for copy in owned_g:
        copy.wait()


def entry_kernel(own, n_time, a_ref, g_ref, e_ref, tile_ref, cos_ref, tau_ref, live_ref, w_ref, c_ref, x_ref, y_ref):
    e = pl.program_id(0)
    slices, _, size, width = a_ref.shape
    live = live_ref[e]
    row_id = lax.broadcasted_iota(jnp.int32, (16, width), 0)
    chi = [jnp.zeros((size, size), jnp.float32) for _ in range(n_time)]
    for m in range(slices):
        ener = e_ref[m].astype(jnp.float32)
        eg = jnp.sum(jnp.where(row_id == e, ener, 0.0), axis=0, keepdims=True)
        ea = jnp.sum(jnp.where(row_id == own + e, ener, 0.0), axis=0, keepdims=True)
        a = a_ref[m, 0].astype(jnp.float32)
        g = g_ref[:, m, 0].reshape(size, width).astype(jnp.float32)
        for t in range(n_time):
            x = (a * jnp.exp(-tau_ref[t] * ea)).astype(jnp.bfloat16)
            y = (g * jnp.exp(-tau_ref[t] * eg)).astype(jnp.bfloat16)
            x_ref[t, m] = x
            y_ref[t, m] = y
            chi[t] = chi[t] + lax.dot_general(
                x, y, (((1,), (1,)), ((), ())), preferred_element_type=jnp.float32
            )
    chi = [c * live for c in chi]
    wfreq = []
    for w in range(n_time):
        chiw = sum(cos_ref[w, t] * chi[t] for t in range(n_time)).astype(jnp.bfloat16)
        prod = jnp.dot(chiw, tile_ref[0], preferred_element_type=jnp.float32)
        prod_b = prod.astype(jnp.bfloat16)
        wfreq.append(
            prod + jnp.dot(prod_b, prod_b, preferred_element_type=jnp.float32) * (1.0 / math.sqrt(size))
        )
    screened = []
    for t in range(n_time):
        wt = (sum(cos_ref[w, t] * wfreq[w] for w in range(n_time)) * (1.0 / n_time)).astype(jnp.bfloat16)
        w_ref[0, t] = wt
        screened.append(wt)
    for m in range(slices):
        total = jnp.zeros((1, width), jnp.float32)
        for t in range(n_time):
            wy = jnp.dot(screened[t], y_ref[t, m], preferred_element_type=jnp.float32)
            total = total + jnp.sum(x_ref[t, m].astype(jnp.float32) * wy, axis=0, keepdims=True)
        c_ref[0, pl.ds(m, 1), :] = total * (1.0 / n_time)


def return_kernel(
    n_tm, n_pair, own,
    back_ref, keep_ref, contrib_ref, owning_ref,
    out_ref,
    c_send, c_recv, p_send, p_recv, tm_sems, pair_sems,
):
    my_tm, my_pair = lax.axis_index("tm"), lax.axis_index("pair")
    peers, others = n_pair - 1, n_tm - 1
    width = out_ref.shape[1]
    c_send[...] = jnp.zeros_like(c_send)
    p_send[...] = jnp.zeros_like(p_send)
    greet(n_tm, n_pair, my_tm, my_pair)

    def stage_c(u):
        owner = lax.rem(my_tm + u + 1, n_tm)
        for e in range(own):
            c_send[u, pl.ds(e, 1), :] = contrib_ref[e, pl.ds(owner, 1), :]
        return owner

    def tm_one(u, carry):
        owner = stage_c(u)
        pltpu.make_async_remote_copy(
            src_ref=c_send.at[u], dst_ref=c_recv.at[u],
            send_sem=tm_sems.at[0], recv_sem=tm_sems.at[1],
            device_id=(owner, my_pair), device_id_type=MESH,
        ).start()
        return carry

    lax.fori_loop(0, others, tm_one, 0)
    stage_c(others)
    wait_bytes(c_recv.at[pl.ds(0, others)], tm_sems.at[1])
    c_recv[others] = c_send[others]

    def stage_p(i):
        for j in range(CAP):
            at = back_ref[CAP * i + j]
            keep = keep_ref[CAP * i + j]
            p_send[i, pl.ds(j, 1), :] = c_recv[at // own, pl.ds(lax.rem(at, own), 1), :] * keep

    def pair_one(i, carry):
        stage_p(i)
        target = lax.rem(my_pair + n_pair - 1 - i, n_pair)
        pltpu.make_async_remote_copy(
            src_ref=p_send.at[i], dst_ref=p_recv.at[i],
            send_sem=pair_sems.at[0], recv_sem=pair_sems.at[1],
            device_id=(my_tm, target), device_id_type=MESH,
        ).start()
        return carry

    lax.fori_loop(0, peers, pair_one, 0)
    stage_p(peers)
    wait_bytes(p_recv.at[pl.ds(0, peers)], pair_sems.at[1])
    p_recv[peers] = p_send[peers]
    incoming = p_recv[...].reshape(n_pair * 8, width)
    out_ref[...] = jnp.dot(
        owning_ref[...], incoming, precision=lax.Precision.HIGHEST, preferred_element_type=jnp.float32
    )
    wait_bytes(c_send.at[pl.ds(0, others)], tm_sems.at[0])
    wait_bytes(p_send.at[pl.ds(0, peers)], pair_sems.at[0])


def body(n_tm, n_pair, coefs, energies, coulomb, tau_grid, freq_grid, pairs):
    blocks, size, width = coefs.shape
    n_time = tau_grid.shape[0]
    listed = pairs.shape[1]
    own = listed // n_tm
    my_tm, my_pair = lax.axis_index("tm"), lax.axis_index("pair")
    remote, local = pairs[:, :, 0], pairs[:, :, 1]
    live = remote >= 0
    source = jnp.where(live, remote // blocks, -1)
    held = remote % blocks
    pos = jnp.arange(listed, dtype=jnp.int32)
    before = (source[:, :, None] == source[:, None, :]) & (pos[None, :] < pos[:, None])[None]
    rank = jnp.sum(before.astype(jnp.int32), axis=2)
    slots = jnp.arange(CAP, dtype=jnp.int32)
    hit = (source == my_pair)[:, None, :] & (rank[:, None, :] == slots[None, :, None])
    pick = jnp.sum(jnp.where(hit, held[:, None, :], 0), axis=2)
    used = jnp.sum(hit.astype(jnp.int32), axis=2)
    turn = lambda v: lax.dynamic_slice_in_dim(jnp.concatenate([v, v]), my_pair + 1, n_pair)
    pick, used = turn(pick), turn(used)
    row = lambda v: lax.dynamic_index_in_dim(v, my_pair, 0, keepdims=False)
    my_live, my_source, my_rank = row(live), row(source), row(rank)
    my_local = jnp.where(my_live, row(local), 0)
    offset = (my_pair - my_source + n_pair - 1) % n_pair
    slot = jnp.where(my_live, offset * CAP + my_rank, 0)
    lane = jnp.arange(n_pair * CAP, dtype=jnp.int32)
    match = (slot[None, :] == lane[:, None]) & my_live[None, :]
    back = jnp.sum(jnp.where(match, pos[None, :], 0), axis=1)
    back_keep = jnp.sum(match.astype(jnp.float32), axis=1)
    back = ((my_tm - back // own + n_tm - 1) % n_tm) * own + back % own
    tall = jnp.arange(8, dtype=jnp.int32)
    pick8 = jnp.pad(jnp.where(used > 0, pick, -1), ((0, 0), (0, 8 - CAP)), constant_values=-1)
    owning = (jnp.arange(blocks, dtype=jnp.int32)[:, None] == pick8.reshape(1, -1)).astype(jnp.float32)
    my_owned = lax.dynamic_slice_in_dim(my_live, my_tm * own, own).astype(jnp.float32)
    cosine = jnp.cos(freq_grid[:, None] * tau_grid[None, :])
    ener16 = jnp.broadcast_to(energies[:, None, :], (blocks, 16, width))

    smem = pl.BlockSpec(memory_space=pltpu.SMEM)
    vmem = pl.BlockSpec(memory_space=pltpu.VMEM)
    hbm = pl.BlockSpec(memory_space=pl.ANY)
    step = size // CHUNKS
    bf16 = jnp.bfloat16
    DMA = pltpu.SemaphoreType.DMA
    a_all, g_all, e_all = pl.pallas_call(
        functools.partial(gather_kernel, n_tm, n_pair, own, size),
        out_shape=(
            jax.ShapeDtypeStruct((n_tm, own, size, width), bf16),
            jax.ShapeDtypeStruct((CHUNKS, n_tm, own, step, width), bf16),
            jax.ShapeDtypeStruct((n_tm, 16, width), bf16),
        ),
        in_specs=[smem] * 3 + [vmem] * 2,
        out_specs=(hbm, hbm, hbm),
        scratch_shapes=[pltpu.VMEM((CAP * n_pair, step, width), bf16)] * (2 * CHUNKS)
        + [
            pltpu.VMEM((n_pair, 16, width), bf16),
            pltpu.VMEM((n_pair, 16, width), bf16),
            pltpu.VMEM((n_tm, own, size, width), bf16),
            pltpu.VMEM((CHUNKS, n_tm, own, step, width), bf16),
            pltpu.VMEM((n_tm, 16, width), bf16),
            DMA((CHUNKS + 1,)),
            DMA((CHUNKS + 1,)),
            DMA((2,)),
            DMA((2, CHUNKS)),
            DMA((2,)),
            DMA((2 + CHUNKS,)),
        ],
        compiler_params=pltpu.CompilerParams(
            collective_id=0, has_side_effects=True, vmem_limit_bytes=56 * 1024 * 1024
        ),
    )(slot, my_local, pick.reshape(-1), coefs, ener16)

    screened, contrib = pl.pallas_call(
        functools.partial(entry_kernel, own, n_time),
        grid=(own,),
        out_shape=(
            jax.ShapeDtypeStruct((own, n_time, size, size), bf16),
            jax.ShapeDtypeStruct((own, n_tm, width), jnp.float32),
        ),
        in_specs=[
            pl.BlockSpec((n_tm, 1, size, width), lambda e: (0, e, 0, 0)),
            pl.BlockSpec((CHUNKS, n_tm, 1, step, width), lambda e: (0, 0, e, 0, 0)),
            pl.BlockSpec((n_tm, 16, width), lambda e: (0, 0, 0)),
            pl.BlockSpec((1, size, size), lambda e: (e, 0, 0)),
            smem, smem, smem,
        ],
        out_specs=(
            pl.BlockSpec((1, n_time, size, size), lambda e: (e, 0, 0, 0)),
            pl.BlockSpec((1, n_tm, width), lambda e: (e, 0, 0)),
        ),
        scratch_shapes=[pltpu.VMEM((n_time, n_tm, size, width), bf16)] * 2,
        compiler_params=pltpu.CompilerParams(vmem_limit_bytes=48 * 1024 * 1024),
    )(a_all, g_all, e_all, coulomb[0], cosine, tau_grid, my_owned)

    self_energy = pl.pallas_call(
        functools.partial(return_kernel, n_tm, n_pair, own),
        out_shape=jax.ShapeDtypeStruct((blocks, width), jnp.float32),
        in_specs=[smem, smem, vmem, vmem],
        out_specs=vmem,
        scratch_shapes=[
            pltpu.VMEM((n_tm, 8, width), jnp.float32),
            pltpu.VMEM((n_tm, 8, width), jnp.float32),
            pltpu.VMEM((n_pair, 8, width), jnp.float32),
            pltpu.VMEM((n_pair, 8, width), jnp.float32),
            DMA((2,)),
            DMA((2,)),
        ],
        compiler_params=pltpu.CompilerParams(collective_id=1, has_side_effects=True),
    )(back, back_keep, contrib, owning)
    return (screened[None], self_energy)


def solution(mesh):
    return jax.shard_map(
        functools.partial(body, mesh.shape["tm"], mesh.shape["pair"]),
        mesh=mesh,
        in_specs=(
            P("pair", None, "tm"),
            P("pair", "tm"),
            P("pair", "tm", None, None),
            P(),
            P(),
            P(),
        ),
        out_specs=(P("pair", "tm", None, None, None), P("pair", "tm")),
        check_vma=False,
    )
```

time: 546 us -> 265 us (0.49)
  waiting for transfers between devices: 402 us -> 0 us
  Pallas kernels: 0 us -> 251 us
  matrix products: 45.4 us -> 0 us
  starting transfers between devices: 31.4 us -> 0 us
  local copies, waits for them, and re-layouts: 32.6 us -> 8.52 us
  between operations: 16.9 us -> 0.75 us
  other arithmetic: 16.6 us -> 4.31 us
    pallas_call x0 -> x3, Pallas kernels: none -> 251 us  [the longest x1 216 us: body(): pl.pallas_call(functools.partial(gather_kernel, n_tm, n_pair, own, size),...]
    all_to_all x3 -> x0, waiting for transfers between devices: 180 us -> none  [the longest x1 172 us: body(): lax.all_to_all(send_coef, 'pair', split_axis=0, concat_axis=0, tiled=True)]
    unnamed x3 -> x0, waiting for transfers between devices: 151 us -> none
    all_gather x1 -> x0, waiting for transfers between devices: 70.6 us -> none  [body(): piece = lax.all_gather(wtime, 'tm', axis=0, tiled=True)]
    dot_general x12 -> x0, matrix products: 45.4 us -> none  [the longest x3 17.5 us: body(): jnp.einsum('kpq,kqm->kpm', piece[:, tpoint], stacked_g[tpoint], preferred...]
    all_to_all x3 -> x0, starting transfers between devices: 31.1 us -> none  [the longest x1 12 us: body(): lax.all_to_all(send_ener, 'pair', split_axis=0, concat_axis=0, tiled=True)]
    gather x7 -> x0, local copies, waits for them, and re-layouts: 23.7 us -> none  [the longest x1 8.76 us: body(): send_coef = coefs[picked] * send_keep[:, None, None]]
    another operation x2 -> x0, other arithmetic: 8.05 us -> none  [the longest x1 7.87 us: body(): partial_value = jnp.stack(partial_list, axis=1)]
  transfers between devices with their start and end apart: 5 -> 0, of which waited for: 4 -> 0; matrix products, arithmetic and copies ran while one was open for 5% -> 0% of each run, Pallas kernels for 0% -> 0%
where the time goes in v1:
time: 265 us
  Pallas kernels  251 us (95%)
  local copies, waits for them, and re-layouts  8.52 us (3%)
  other arithmetic  4.31 us (2%)
    pallas_call x1, Pallas kernels, body(): pl.pallas_call(functools.partial(gather_kernel, n_tm, n_pair, own, size),...  216 us
    pallas_call x1, Pallas kernels, body(): pl.pallas_call(functools.partial(return_kernel, n_tm, n_pair, own), out_s...  20.4 us
    pallas_call x1, Pallas kernels, body(): pl.pallas_call(functools.partial(entry_kernel, own, n_time), grid=(own,),...  14.6 us

profile of v1, /device:TPU:1, one launch (start us, length us, event | category | flops | bytes accessed | tf_op | source)
XLA Modules:
  0.0 264.8 jit_solution(9266110184618449700)
XLA Ops:
  0.6 0.9 fusion.30
  1.6 0.8 convert_reduce_fusion
  2.4 0.1 convert_reduce_fusion.1
  2.5 0.1 pad_add_fusion
  2.6 0.1 compare_select_fusion.6
  2.7 0.1 copy.11
  2.8 0.7 reshape.100.pick_ref
  3.5 0.5 fusion.14
  4.0 0.5 fusion.17.slot_ref
  4.5 1.6 broadcast_in_dim.39.ener_ref
  6.1 0.0 copy-start.4
  6.1 0.0 copy-start.5
  6.1 0.0 copy-start.1
  6.1 216.2 %shard_map.77 = (bf16[8,4,256,256]{3,2,1,0:T(8,128)(2,1)}, bf16[4,8,4,64,256]{4,3,2,1,0:T(8,128)(2,1)}, bf16[8,16,256]{2,1,0:T(8,128)(2,1)}) custom-call(s32[32]{0:T(128)} %fusion.17.slot_ref, s32[32]{0:T(128)} %get-tuple-element.18.local_ref, s32[64]{0:T(128)} %reshape.100.pick_ref, bf16[64,256,256]{2,1,0:T(8,128)(2,1)} %coef_ref.1, ...), custom_call_target="tpu_custom_call" | custom-call | tf_op jit(solution)/shard_map/pallas_call | solution.py:331
  222.3 0.1 fusion.18.live_ref
  222.4 0.0 copy-done.4
  222.4 0.0 copy-done.5
  222.4 0.1 multiply_cosine_fusion.cos_ref
  222.5 0.0 copy-done.1
  222.5 0.0 copy-start
  222.5 2.2 copy-done
  224.7 0.0 copy-start.2
  224.7 0.8 copy-done.2
  225.6 14.6 %shard_map.78 = (bf16[4,3,256,256]{3,2,1,0:T(8,128)(2,1)}, f32[4,8,256]{2,1,0:T(8,128)S(1)}) custom-call(bf16[8,4,256,256]{3,2,1,0:T(8,128)(2,1)S(1)} %copy-done, bf16[4,8,4,64,256]{4,3,2,1,0:T(8,128)(2,1)} %get-tuple-element.8.g_ref, bf16[8,16,256]{2,1,0:T(8,128)(2,1)S(1)} %copy-done.2, bf16[4,256,256]{2,1,0:T(8,128)(2,1)S(1)} %bitcast.22, ...), custom_call_target="tpu_custom_call" | custom-call | tf_op jit(solution)/shard_map/pallas_call | solution.py:359
  240.2 0.0 copy-start.3
  240.2 0.6 copy-done.3
  240.8 0.1 select_reduce_fusion.1
  240.9 0.5 fusion.10.back_ref
  241.4 0.7 convert_reduce_fusion.2.keep_ref
  242.1 0.1 copy.14
  242.2 0.1 eq.89
  242.3 0.6 fusion.owning_ref
  242.9 20.4 %shard_map.79 = f32[64,256]{1,0:T(8,128)} custom-call(s32[64]{0:T(128)} %fusion.10.back_ref, f32[64]{0:T(128)} %convert_reduce_fusion.2.keep_ref, f32[4,8,256]{2,1,0:T(8,128)} %copy-done.3, f32[64,256]{1,0:T(8,128)} %fusion.owning_ref), custom_call_target="tpu_custom_call" | custom-call | tf_op jit(solution)/shard_map/pallas_call | solution.py:381
  263.3 1.5 copy.16
  (6 shorter events, 0.1 us)
Async XLA Ops:
  6.1 216.3 %copy-start.4 = (f32[3]{0:T(128)S(1)}, f32[3]{0:T(128)}, u32[]{:S(2)}) copy-start(f32[3]{0:T(128)} %tau_ref.1) | copy-start | bytes 40
  6.1 216.3 %copy-start.5 = (f32[3]{0:T(128)S(1)}, f32[3]{0:T(128)}, u32[]{:S(2)}) copy-start(f32[3]{0:T(128)} %param.10) | copy-start | bytes 40
  6.1 216.5 %copy-start.1 = (bf16[1,4,256,256]{3,2,1,0:T(8,128)(2,1)S(1)}, bf16[1,4,256,256]{3,2,1,0:T(8,128)(2,1)}, u32[]{:S(2)}) copy-start(bf16[1,4,256,256]{3,2,1,0:T(8,128)(2,1)} %param.8) | copy-start | bytes 1572868
  222.5 2.2 copy-start
  224.7 0.8 copy-start.2
  240.2 0.6 copy-start.3

commit v2 on v1

--- a/solution.py
+++ b/solution.py
@@ -10,6 +10,11 @@
 
 CAP = 2
 CHUNKS = 4
+FAST_CHUNKS = 8
+Y_CAP = 15
+Z_CAPS = (11, 11, 10, 9)
+N_Y = 4
+POOLS = 3
 MESH = pl.DeviceIdType.MESH
 
 
@@ -128,7 +133,7 @@
         def g_one(u, carry):
             owner = stage_g(u)
             pltpu.make_async_remote_copy(
-                src_ref=g_send.at[c, u], dst_ref=g_out.at[c, my_tm],
+                src_ref=g_send.at[c, u], dst_ref=g_out.at[my_tm, :, pl.ds(c * step, step)],
                 send_sem=g_sems.at[0, c], recv_sem=g_sems.at[1, c],
                 device_id=(owner, my_pair), device_id_type=MESH,
             ).start()
@@ -136,7 +141,7 @@
 
         lax.fori_loop(0, others, g_one, 0)
         stage_g(others)
-        copy = pltpu.make_async_copy(g_send.at[c, others], g_out.at[c, my_tm], own_sems.at[1 + c])
+        copy = pltpu.make_async_copy(g_send.at[c, others], g_out.at[my_tm, :, pl.ds(c * step, step)], own_sems.at[1 + c])
         copy.start()
         owned_g.append(copy)
         if c == 0:
@@ -183,6 +188,306 @@
         copy.wait()
 
 
+def fast_kernel(
+    n_tm, n_pair, own, rows,
+    final_ref, slot_ref, local_ref, pick_ref, y_ref, z_ref, coef_ref, ener_ref,
+    a_out, g_out, e_out,
+    y_send, y_recv, z_send, z_recv, e_send, e_recv, x_send, x_ener, *rest,
+):
+    pools = rest[:POOLS]
+    (y_ssem, y_rsem, z_ssem, z_rsem, pair_send, pair_recv, a_sems, g_sems, e_sems, own_sems) = rest[POOLS:]
+    my_tm, my_pair = lax.axis_index("tm"), lax.axis_index("pair")
+    peers, others = n_pair - 1, n_tm - 1
+    n_z = n_pair // N_Y
+    my_y, my_z = my_pair // n_z, lax.rem(my_pair, n_z)
+    step = rows // FAST_CHUNKS
+    blocks = coef_ref.shape[0]
+    y_slots = (N_Y - 1) * Y_CAP
+    ahead = (my_y * n_z + lax.rem(my_z + 1, n_z), my_y * n_z + lax.rem(my_z + n_z - 1, n_z))
+    firsts = [sum(Z_CAPS[:r]) for r in range(len(Z_CAPS) + 1)]
+    greet(n_tm, n_pair, my_tm, my_pair)
+    row_id = lax.broadcasted_iota(jnp.int32, (16, ener_ref.shape[2]), 0)
+
+    def ener_copy(i):
+        target = lax.rem(my_pair + i + 1, n_pair)
+        return pltpu.make_async_remote_copy(
+            src_ref=e_send.at[i], dst_ref=e_recv.at[i],
+            send_sem=pair_send, recv_sem=pair_recv,
+            device_id=(my_tm, target), device_id_type=MESH,
+        )
+
+    def stage_ener(i):
+        tile = jnp.zeros(row_id.shape, jnp.float32)
+        for j in range(CAP):
+            tile = jnp.where(row_id == j, ener_ref[pick_ref[CAP * i + j]].astype(jnp.float32), tile)
+        return tile.astype(jnp.bfloat16)
+
+    def send_ener(i, carry):
+        e_send[i] = stage_ener(i)
+        ener_copy(i).start()
+        return carry
+
+    def send_y(c):
+        for i in range(N_Y - 1):
+            def one(j, carry):
+                y_send[c, i, j] = coef_ref[y_ref[i * Y_CAP + j], pl.ds(c * step, step), :]
+                return carry
+
+            lax.fori_loop(0, Y_CAP, one, 0)
+            target = lax.rem(my_y + i + 1, N_Y) * n_z + my_z
+            pltpu.make_async_remote_copy(
+                src_ref=y_send.at[c, i], dst_ref=y_recv.at[c, i],
+                send_sem=y_ssem, recv_sem=y_rsem.at[c],
+                device_id=(my_tm, target), device_id_type=MESH,
+            ).start()
+
+    def fill(c):
+        pool = pools[c % POOLS]
+        pool[pl.ds(0, blocks)] = coef_ref[:, pl.ds(c * step, step), :]
+        wait_bytes(y_recv.at[c], y_rsem.at[c])
+        for i in range(N_Y - 1):
+            pool[pl.ds(blocks + i * Y_CAP, Y_CAP)] = y_recv[c, i]
+
+    def span(c, r, way):
+        return (c, way, pl.ds(firsts[r], Z_CAPS[r]))
+
+    def send_z(c, r):
+        pool = pools[c % POOLS]
+        for way in range(2):
+            base = (2 * r + way) * Z_CAPS[0]
+
+            def one(j, carry):
+                z_send[c, way, firsts[r] + j] = pool[z_ref[base + j]]
+                return carry
+
+            lax.fori_loop(0, Z_CAPS[r], one, 0)
+            pltpu.make_async_remote_copy(
+                src_ref=z_send.at[span(c, r, way)], dst_ref=z_recv.at[span(c, r, way)],
+                send_sem=z_ssem, recv_sem=z_rsem.at[c, r, way],
+                device_id=(my_tm, ahead[way]), device_id_type=MESH,
+            ).start()
+
+    def take_z(c, r):
+        pool = pools[c % POOLS]
+        for way in range(2):
+            wait_bytes(z_recv.at[span(c, r, way)], z_rsem.at[c, r, way])
+            at = blocks + y_slots + way * firsts[-1] + firsts[r]
+            pool[pl.ds(at, Z_CAPS[r])] = z_recv[span(c, r, way)]
+
+    def stage_a(u):
+        owner = lax.rem(my_tm + u + 1, n_tm)
+        for e in range(own):
+            x_send[u, e] = coef_ref[local_ref[owner * own + e]]
+        return owner
+
+    def a_one(u, carry):
+        owner = stage_a(u)
+        pltpu.make_async_remote_copy(
+            src_ref=x_send.at[u], dst_ref=a_out.at[my_tm],
+            send_sem=a_sems.at[0], recv_sem=a_sems.at[1],
+            device_id=(owner, my_pair), device_id_type=MESH,
+        ).start()
+        return carry
+
+    def send_x(c):
+        pool = pools[c % POOLS]
+        part = pl.ds(c * step, step)
+
+        def stage_g(u):
+            owner = lax.rem(my_tm + u + 1, n_tm)
+            for e in range(own):
+                x_send[u, e, part] = pool[final_ref[owner * own + e]]
+            return owner
+
+        def g_one(u, carry):
+            owner = stage_g(u)
+            pltpu.make_async_remote_copy(
+                src_ref=x_send.at[u, :, part], dst_ref=g_out.at[my_tm, :, part],
+                send_sem=g_sems.at[0, c], recv_sem=g_sems.at[1, c],
+                device_id=(owner, my_pair), device_id_type=MESH,
+            ).start()
+            return carry
+
+        lax.fori_loop(0, others, g_one, 0)
+        stage_g(others)
+        pltpu.make_async_copy(x_send.at[others, :, part], g_out.at[my_tm, :, part], own_sems.at[1 + c]).start()
+
+    def send_x_ener():
+        wait_bytes(e_recv.at[pl.ds(0, peers)], pair_recv)
+
+        def stage_x(u):
+            owner = lax.rem(my_tm + u + 1, n_tm)
+            tile = jnp.zeros(row_id.shape, jnp.float32)
+            for e in range(own):
+                slot = slot_ref[owner * own + e]
+                held = e_recv[slot // CAP].astype(jnp.float32)
+                picked = jnp.sum(jnp.where(row_id == lax.rem(slot, CAP), held, 0.0), axis=0, keepdims=True)
+                tile = jnp.where(row_id == e, picked, tile)
+                mine = ener_ref[local_ref[owner * own + e]].astype(jnp.float32)
+                tile = jnp.where(row_id == own + e, mine, tile)
+            x_ener[u] = tile.astype(jnp.bfloat16)
+            return owner
+
+        def x_one(u, carry):
+            owner = stage_x(u)
+            pltpu.make_async_remote_copy(
+                src_ref=x_ener.at[u], dst_ref=e_out.at[my_tm],
+                send_sem=e_sems.at[0], recv_sem=e_sems.at[1],
+                device_id=(owner, my_pair), device_id_type=MESH,
+            ).start()
+            return carry
+
+        lax.fori_loop(0, others, x_one, 0)
+        stage_x(others)
+        pltpu.make_async_copy(x_ener.at[others], e_out.at[my_tm], own_sems.at[1 + FAST_CHUNKS]).start()
+
+    send_y(0)
+    lax.fori_loop(0, peers, send_ener, 0)
+    e_recv[peers] = stage_ener(peers)
+    send_y(1)
+    lax.fori_loop(0, others, a_one, 0)
+    stage_a(others)
+    own_a = pltpu.make_async_copy(x_send.at[others], a_out.at[my_tm], own_sems.at[0])
+    own_a.start()
+    last = len(Z_CAPS) - 1
+    fill(0)
+    send_z(0, 0)
+    fill(1)
+    send_z(1, 0)
+    for first in range(0, FAST_CHUNKS, 2):
+        second = first + 1
+        more = first + 2 < FAST_CHUNKS
+        if more:
+            send_y(first + 2)
+        for r in range(last):
+            take_z(first, r)
+            send_z(first, r + 1)
+            take_z(second, r)
+            send_z(second, r + 1)
+            if more and r == 0:
+                send_y(first + 3)
+        if more:
+            fill(first + 2)
+            send_z(first + 2, 0)
+        take_z(first, last)
+        if first == 0:
+            own_a.wait()
+            wait_bytes(x_send.at[pl.ds(0, others)], a_sems.at[0])
+        send_x(first)
+        if more:
+            fill(first + 3)
+            send_z(first + 3, 0)
+        take_z(second, last)
+        send_x(second)
+        if first == 0:
+            send_x_ener()
+
+    wait_bytes(y_send, y_ssem)
+    wait_bytes(z_send, z_ssem)
+    wait_bytes(e_send.at[pl.ds(0, peers)], pair_send)
+    wait_bytes(x_send.at[pl.ds(0, others)], a_sems.at[1])
+    for side in range(2):
+        wait_bytes(x_ener.at[pl.ds(0, others)], e_sems.at[side])
+        for c in range(FAST_CHUNKS):
+            wait_bytes(x_send.at[pl.ds(0, others), :, pl.ds(c * step, step)], g_sems.at[side, c])
+    for c in range(FAST_CHUNKS):
+        part = pl.ds(c * step, step)
+        pltpu.make_async_copy(x_send.at[others, :, part], g_out.at[my_tm, :, part], own_sems.at[1 + c]).wait()
+    pltpu.make_async_copy(x_ener.at[others], e_out.at[my_tm], own_sems.at[1 + FAST_CHUNKS]).wait()
+
+
+def list_fits(n_pair, live, source):
+    n_z = n_pair // N_Y
+    ids = jnp.arange(n_pair, dtype=jnp.int32)
+    count = jnp.sum((source[:, :, None] == ids).astype(jnp.int32), axis=1)
+    by_y = jnp.sum(count.reshape(N_Y, n_z, N_Y, n_z), axis=1)
+    far = jnp.arange(N_Y)[:, None, None] != jnp.arange(N_Y)[None, :, None]
+    fits = jnp.all(jnp.where(far, by_y, 0) <= Y_CAP)
+    at = jnp.sum(count.reshape(N_Y, n_z, N_Y, n_z), axis=2)
+    half = n_z // 2
+    y_id, z_id = jnp.arange(N_Y)[:, None], jnp.arange(n_z)[None, :]
+    zd_id, zs_id = jnp.arange(n_z)[:, None], jnp.arange(n_z)[None, :]
+    delta = (zd_id - zs_id) % n_z
+    for way in range(2):
+        queue = [None]
+        for far_by in range(1, half + 1):
+            gap = far_by if way == 0 else n_z - far_by
+            n = jnp.sum(jnp.where(delta[None] == gap, at, 0), axis=1)
+            if far_by == half:
+                even = (y_id + z_id) % 2 == 0
+                n = (n + jnp.where(even, 1 - way, way)) // 2
+            queue.append(n)
+        for cap in Z_CAPS:
+            left = jnp.full((N_Y, n_z), cap, jnp.int32)
+            moved = [None] * (half + 1)
+            for far_by in range(half, 0, -1):
+                moved[far_by] = jnp.minimum(queue[far_by], left)
+                left = left - moved[far_by]
+            for far_by in range(1, half + 1):
+                queue[far_by] = queue[far_by] - moved[far_by]
+                if far_by < half:
+                    queue[far_by] = queue[far_by] + jnp.roll(moved[far_by + 1], 1 - 2 * way, axis=1)
+        fits = fits & (sum(jnp.sum(q) for q in queue[1:]) == 0)
+    return fits
+
+
+def routes(n_pair, blocks, my_pair, live, source, held, rank):
+    listed = live.shape[1]
+    n_z = n_pair // N_Y
+    my_y, my_z = my_pair // n_z, my_pair % n_z
+    rows = jnp.arange(n_pair, dtype=jnp.int32)
+    mine = source == my_pair
+    per_row = jnp.sum(mine.astype(jnp.int32), axis=1)
+    same = (rows[:, None] // n_z == rows[None, :] // n_z) & (rows[None, :] < rows[:, None])
+    first = jnp.sum(jnp.where(same, per_row[None, :], 0), axis=1)
+    place = jnp.where(mine, first[:, None] + rank, -1).reshape(N_Y, 1, n_z * listed)
+    want = jnp.arange(Y_CAP, dtype=jnp.int32)[None, :, None]
+    y_tab = jnp.sum(jnp.where(place == want, held.reshape(N_Y, 1, n_z * listed), 0), axis=2)
+    y_tab = lax.dynamic_slice_in_dim(jnp.concatenate([y_tab, y_tab]), my_y + 1, N_Y - 1)
+
+    ring = lambda v: lax.dynamic_slice_in_dim(v, my_y * n_z, n_z).reshape(n_z * listed)
+    src, hold, alive = ring(source), ring(held), ring(live)
+    n = n_z * listed
+    ids = jnp.arange(n, dtype=jnp.int32)
+    zd = ids // listed
+    ys, zs = src // n_z, src % n_z
+    earlier = ids[None, :] < ids[:, None]
+    y_rank = jnp.sum(((src[:, None] == src[None, :]) & earlier).astype(jnp.int32), axis=1)
+    z_key = jnp.where(alive, zs, -1)
+    z_rank = jnp.sum(
+        ((z_key[:, None] == z_key[None, :]) & (zd[:, None] == zd[None, :]) & earlier).astype(jnp.int32), axis=1
+    )
+    step_y = (my_y - ys) % N_Y
+    loc = jnp.where(step_y == 0, hold, blocks + (step_y - 1) * Y_CAP + y_rank)
+    loc = jnp.where(alive, loc, 0)
+    delta = (zd - zs) % n_z
+    half = n_z // 2
+    plus = (delta < half) | ((delta == half) & ((z_rank + zs + my_y) % 2 == 0))
+    way = jnp.where(plus, 0, 1)
+    rem = jnp.where(alive, jnp.where(plus, delta, n_z - delta), 0)
+    pos = zs
+    total = sum(Z_CAPS)
+    tables, begun = [], 0
+    slots = jnp.arange(Z_CAPS[0], dtype=jnp.int32)
+    for cap in Z_CAPS:
+        active = rem > 0
+        group = jnp.where(active, pos * 2 + way, -1)
+        key = rem * n - ids
+        ahead = (group[:, None] == group[None, :]) & (key[None, :] > key[:, None])
+        order = jnp.sum(ahead.astype(jnp.int32), axis=1)
+        moved = active & (order < cap)
+        for w in range(2):
+            here = jnp.where(moved & (group == my_z * 2 + w), order, -1)
+            tables.append(jnp.sum(jnp.where(here[None, :] == slots[:, None], loc[None, :], 0), axis=1))
+        to = blocks + (N_Y - 1) * Y_CAP + way * total + begun + order
+        loc = jnp.where(moved, to, loc)
+        pos = jnp.where(moved, (pos + jnp.where(plus, 1, n_z - 1)) % n_z, pos)
+        rem = rem - moved.astype(jnp.int32)
+        begun += cap
+    final = lax.dynamic_slice_in_dim(loc, my_z * listed, listed)
+    return y_tab.reshape(-1), jnp.concatenate(tables), final
+
+
 def entry_kernel(own, n_time, a_ref, g_ref, e_ref, tile_ref, cos_ref, tau_ref, live_ref, w_ref, c_ref, x_ref, y_ref):
     e = pl.program_id(0)
     slices, _, size, width = a_ref.shape
@@ -194,7 +499,7 @@
         eg = jnp.sum(jnp.where(row_id == e, ener, 0.0), axis=0, keepdims=True)
         ea = jnp.sum(jnp.where(row_id == own + e, ener, 0.0), axis=0, keepdims=True)
         a = a_ref[m, 0].astype(jnp.float32)
-        g = g_ref[:, m, 0].reshape(size, width).astype(jnp.float32)
+        g = g_ref[m, 0].astype(jnp.float32)
         for t in range(n_time):
             x = (a * jnp.exp(-tau_ref[t] * ea)).astype(jnp.bfloat16)
             y = (g * jnp.exp(-tau_ref[t] * eg)).astype(jnp.bfloat16)
@@ -325,36 +630,81 @@
     smem = pl.BlockSpec(memory_space=pltpu.SMEM)
     vmem = pl.BlockSpec(memory_space=pltpu.VMEM)
     hbm = pl.BlockSpec(memory_space=pl.ANY)
-    step = size // CHUNKS
     bf16 = jnp.bfloat16
     DMA = pltpu.SemaphoreType.DMA
-    a_all, g_all, e_all = pl.pallas_call(
-        functools.partial(gather_kernel, n_tm, n_pair, own, size),
-        out_shape=(
-            jax.ShapeDtypeStruct((n_tm, own, size, width), bf16),
-            jax.ShapeDtypeStruct((CHUNKS, n_tm, own, step, width), bf16),
-            jax.ShapeDtypeStruct((n_tm, 16, width), bf16),
-        ),
-        in_specs=[smem] * 3 + [vmem] * 2,
-        out_specs=(hbm, hbm, hbm),
-        scratch_shapes=[pltpu.VMEM((CAP * n_pair, step, width), bf16)] * (2 * CHUNKS)
-        + [
-            pltpu.VMEM((n_pair, 16, width), bf16),
-            pltpu.VMEM((n_pair, 16, width), bf16),
-            pltpu.VMEM((n_tm, own, size, width), bf16),
-            pltpu.VMEM((CHUNKS, n_tm, own, step, width), bf16),
-            pltpu.VMEM((n_tm, 16, width), bf16),
-            DMA((CHUNKS + 1,)),
-            DMA((CHUNKS + 1,)),
-            DMA((2,)),
-            DMA((2, CHUNKS)),
-            DMA((2,)),
-            DMA((2 + CHUNKS,)),
-        ],
-        compiler_params=pltpu.CompilerParams(
-            collective_id=0, has_side_effects=True, vmem_limit_bytes=56 * 1024 * 1024
-        ),
-    )(slot, my_local, pick.reshape(-1), coefs, ener16)
+    step = size // CHUNKS
+    thin = size // FAST_CHUNKS
+    gathered = (
+        jax.ShapeDtypeStruct((n_tm, own, size, width), bf16),
+        jax.ShapeDtypeStruct((n_tm, own, size, width), bf16),
+        jax.ShapeDtypeStruct((n_tm, 16, width), bf16),
+    )
+    fits = list_fits(n_pair, live, source)
+    y_tab, z_tab, final = routes(n_pair, blocks, my_pair, live, source, held, rank)
+    pick_flat = pick.reshape(-1)
+
+    def pooled(slot, my_local, pick_flat, y_tab, z_tab, final, coefs, ener16):
+        total = sum(Z_CAPS)
+        depth = blocks + (N_Y - 1) * Y_CAP + 2 * total
+        return pl.pallas_call(
+            functools.partial(fast_kernel, n_tm, n_pair, own, size),
+            out_shape=gathered,
+            in_specs=[smem] * 6 + [vmem] * 2,
+            out_specs=(hbm, hbm, hbm),
+            scratch_shapes=[pltpu.VMEM((FAST_CHUNKS, N_Y - 1, Y_CAP, thin, width), bf16)] * 2
+            + [pltpu.VMEM((FAST_CHUNKS, 2, total, thin, width), bf16)] * 2
+            + [
+                pltpu.VMEM((n_pair, 16, width), bf16),
+                pltpu.VMEM((n_pair, 16, width), bf16),
+                pltpu.VMEM((n_tm, own, size, width), bf16),
+                pltpu.VMEM((n_tm, 16, width), bf16),
+            ]
+            + [pltpu.VMEM((depth, thin, width), bf16)] * POOLS
+            + [
+                DMA,
+                DMA((FAST_CHUNKS,)),
+                DMA,
+                DMA((FAST_CHUNKS, len(Z_CAPS), 2)),
+                DMA,
+                DMA,
+                DMA((2,)),
+                DMA((2, FAST_CHUNKS)),
+                DMA((2,)),
+                DMA((2 + FAST_CHUNKS,)),
+            ],
+            compiler_params=pltpu.CompilerParams(
+                collective_id=2, has_side_effects=True, vmem_limit_bytes=62 * 1024 * 1024
+            ),
+        )(final, slot, my_local, pick_flat, y_tab, z_tab, coefs, ener16)
+
+    def direct(slot, my_local, pick_flat, y_tab, z_tab, final, coefs, ener16):
+        return pl.pallas_call(
+            functools.partial(gather_kernel, n_tm, n_pair, own, size),
+            out_shape=gathered,
+            in_specs=[smem] * 3 + [vmem] * 2,
+            out_specs=(hbm, hbm, hbm),
+            scratch_shapes=[pltpu.VMEM((CAP * n_pair, step, width), bf16)] * (2 * CHUNKS)
+            + [
+                pltpu.VMEM((n_pair, 16, width), bf16),
+                pltpu.VMEM((n_pair, 16, width), bf16),
+                pltpu.VMEM((n_tm, own, size, width), bf16),
+                pltpu.VMEM((CHUNKS, n_tm, own, step, width), bf16),
+                pltpu.VMEM((n_tm, 16, width), bf16),
+                DMA((CHUNKS + 1,)),
+                DMA((CHUNKS + 1,)),
+                DMA((2,)),
+                DMA((2, CHUNKS)),
+                DMA((2,)),
+                DMA((2 + CHUNKS,)),
+            ],
+            compiler_params=pltpu.CompilerParams(
+                collective_id=0, has_side_effects=True, vmem_limit_bytes=56 * 1024 * 1024
+            ),
+        )(slot, my_local, pick_flat, coefs, ener16)
+
+    a_all, g_all, e_all = lax.cond(
+        fits, pooled, direct, slot, my_local, pick_flat, y_tab, z_tab, final, coefs, ener16
+    )
 
     screened, contrib = pl.pallas_call(
         functools.partial(entry_kernel, own, n_time),
@@ -365,7 +715,7 @@
         ),
         in_specs=[
             pl.BlockSpec((n_tm, 1, size, width), lambda e: (0, e, 0, 0)),
-            pl.BlockSpec((CHUNKS, n_tm, 1, step, width), lambda e: (0, 0, e, 0, 0)),
+            pl.BlockSpec((n_tm, 1, size, width), lambda e: (0, e, 0, 0)),
             pl.BlockSpec((n_tm, 16, width), lambda e: (0, 0, 0)),
             pl.BlockSpec((1, size, size), lambda e: (e, 0, 0)),
             smem, smem, smem,

time: 265 us -> 225 us (0.85)
  Pallas kernels: 251 us -> 198 us
  other arithmetic: 4.31 us -> 11.8 us
  between operations: 0.75 us -> 6.7 us
    pallas_call x1, Pallas kernels: 216 us -> 165 us  [pooled(): pl.pallas_call(functools.partial(fast_kernel, n_tm, n_pair, own, size), o...]
    reduce_sum x0 -> x21, other arithmetic: none -> 6.92 us  [the longest x6 4.44 us: list_fits(): fits = fits & (sum((jnp.sum(q) for q in queue[1:])) == 0)]
    unnamed x14 -> x10, local copies, waits for them, and re-layouts: 5.18 us -> 2.17 us
where the time goes in v2:
time: 225 us; the launch traced here: 224 us
  Pallas kernels  198 us (88%)
  other arithmetic  11.8 us (5%)
  local copies, waits for them, and re-layouts  8.04 us (4%)
  between operations  6.7 us (3%)
    pallas_call x1, Pallas kernels, pooled(): pl.pallas_call(functools.partial(fast_kernel, n_tm, n_pair, own, size), o...  165 us
    pallas_call x1, Pallas kernels, body(): pl.pallas_call(functools.partial(return_kernel, n_tm, n_pair, own), out_s...  18.4 us
    pallas_call x1, Pallas kernels, body(): pl.pallas_call(functools.partial(entry_kernel, own, n_time), grid=(own,),...  14.8 us

profile of v2, /device:TPU:1, one launch (start us, length us, event | category | flops | bytes accessed | tf_op | source)
XLA Modules:
  0.0 224.3 jit_solution(9338488153886849833)
XLA Ops:
  0.7 0.9 fusion.100
  1.5 0.1 convert_reduce_fusion.10
  1.8 0.1 reshape.1314
  1.9 0.2 convert_reduce_fusion.7
  2.1 0.2 convert_reduce_fusion.6
  2.4 0.2 convert_reduce_fusion.5
  2.7 0.2 convert_reduce_fusion.4
  2.9 0.2 convert_reduce_fusion.2
  3.2 0.2 convert_reduce_fusion.3
  3.4 0.1 select_reduce_fusion.3
  3.5 0.1 select_reduce_fusion.5
  3.7 0.1 select_reduce_fusion.7
  3.8 0.1 select_reduce_fusion.9
  3.9 0.1 concatenate.112
  4.0 0.8 convert_reduce_fusion
  4.9 0.2 select_reduce_fusion.11
  5.1 0.1 add.1404
  5.2 0.1 add.1406
  5.5 0.3 select_reduce_fusion
  5.9 0.2 convert_reduce_fusion.8
  6.2 0.1 copy.16
  6.3 0.1 reshape.1313
  6.4 0.8 broadcast_in_dim.304
  7.3 0.1 reshape.1312
  7.9 0.7 subtract_reduce_fusion
  9.0 0.7 subtract_reduce_fusion.1
  9.8 0.1 add_add_fusion.1
  10.3 0.7 fusion.38
  11.3 0.8 fusion.42
  14.9 0.8 fusion.36
  16.0 0.7 fusion.43
  19.3 0.7 fusion.16
  20.7 166.0 %conditional.1 = ((bf16[8,4,256,256]{3,2,1,0:T(8,128)(2,1)}, bf16[8,4,256,256]{3,2,1,0:T(8,128)(2,1)}, bf16[8,16,256]{2,1,0:T(8,128)(2,1)S(1)})) conditional(s32[]{:T(128)} %convert_element_type.177, (s32[32]{0:T(128)S(1)}, s32[32]{0:T(128)S(1)}, s32[64]{0:T(128)S(1)}, bf16[64,256,256]{2,1,0:T(8,128)(2,1)}, ...), branch_computations={%region_38.39_spmd, %region_39.40_spmd} | conditional | flops 5896 | bytes 18428 | solution.py:705
  20.8 0.6 dynamic_slice.34.final_ref
  21.5 0.6 reshape.1306.y_ref
  22.1 164.6 %branch_1_fun.3 = (bf16[8,4,256,256]{3,2,1,0:T(8,128)(2,1)}, bf16[8,4,256,256]{3,2,1,0:T(8,128)(2,1)}, bf16[8,16,256]{2,1,0:T(8,128)(2,1)S(1)}) custom-call(s32[32]{0:T(128)} %dynamic_slice.34.final_ref, s32[32]{0:T(128)S(1)} %get-tuple-element.311.slot_ref, s32[32]{0:T(128)S(1)} %get-tuple-element.312.local_ref, s32[64]{0:T(128)S(1)} %get-tuple-element.313.pick_ref, ...), custom_call_target="tpu_custom_call" | custom-call | tf_op jit(solution)/shard_map/cond/branch_1_fun/pallas_call | solution.py:649
  186.7 0.1 fusion.67.live_ref
  186.8 0.1 multiply_cosine_fusion.cos_ref
  186.9 14.8 %shard_map.77 = (bf16[4,3,256,256]{3,2,1,0:T(8,128)(2,1)}, f32[4,8,256]{2,1,0:T(8,128)S(1)}) custom-call(bf16[8,4,256,256]{3,2,1,0:T(8,128)(2,1)} %get-tuple-element.326.a_ref, bf16[8,4,256,256]{3,2,1,0:T(8,128)(2,1)} %get-tuple-element.327.g_ref, bf16[8,16,256]{2,1,0:T(8,128)(2,1)S(1)} %get-tuple-element.328.e_ref, bf16[4,256,256]{2,1,0:T(8,128)(2,1)S(1)} %bitcast.48, ...), custom_call_target="tpu_custom_call" | custom-call | tf_op jit(solution)/shard_map/pallas_call | solution.py:709
  201.7 0.6 copy-done.1
  202.3 0.1 copy.22
  202.4 0.1 eq.775
  202.5 0.6 fusion.6.owning_ref
  203.1 0.1 select_reduce_fusion.2
  203.2 0.5 fusion.63.back_ref
  203.8 0.7 convert_reduce_fusion.9.keep_ref
  204.5 18.4 %shard_map.78 = f32[64,256]{1,0:T(8,128)} custom-call(s32[64]{0:T(128)} %fusion.63.back_ref, f32[64]{0:T(128)} %convert_reduce_fusion.9.keep_ref, f32[4,8,256]{2,1,0:T(8,128)} %copy-done.1, f32[64,256]{1,0:T(8,128)} %fusion.6.owning_ref), custom_call_target="tpu_custom_call" | custom-call | tf_op jit(solution)/shard_map/pallas_call | solution.py:731
  222.8 1.5 copy.30
  (86 shorter events, 3.4 us)
Async XLA Ops:
  20.7 166.1 %copy-start.2 = (f32[3]{0:T(128)S(1)}, f32[3]{0:T(128)}, u32[]{:S(2)}) copy-start(f32[3]{0:T(128)} %tau_ref.1) | copy-start | bytes 40
  20.7 166.1 %copy-start.3 = (f32[3]{0:T(128)S(1)}, f32[3]{0:T(128)}, u32[]{:S(2)}) copy-start(f32[3]{0:T(128)} %param.12) | copy-start | bytes 40
  20.7 166.2 %copy-start = (bf16[1,4,256,256]{3,2,1,0:T(8,128)(2,1)S(1)}, bf16[1,4,256,256]{3,2,1,0:T(8,128)(2,1)}, u32[]{:S(2)}) copy-start(bf16[1,4,256,256]{3,2,1,0:T(8,128)(2,1)} %param.10) | copy-start | bytes 1572868
  201.7 0.6 copy-start.1

commit v3 on v2

--- a/solution.py
+++ b/solution.py
@@ -10,9 +10,11 @@
 
 CAP = 2
 CHUNKS = 4
-FAST_CHUNKS = 8
+PARTS = (16, 16, 32, 32, 32, 32, 32, 32, 16, 16)
+FAST_CHUNKS = len(PARTS)
 Y_CAP = 15
-Z_CAPS = (11, 11, 10, 9)
+Z_CAPS = (10, 10, 10, 9)
+LINE = 128
 N_Y = 4
 POOLS = 3
 MESH = pl.DeviceIdType.MESH
@@ -36,16 +38,31 @@
     pl.semaphore_wait(barrier, n_pair + n_tm - 2)
 
 
+class View:
+    def __init__(self, ref, at):
+        self.ref, self.at = ref, at
+
+    def __getitem__(self, i):
+        return self.ref[self.at + i]
+
+
+def views(table, listed, n_pair):
+    sizes = (listed, listed, CAP * n_pair, listed, (N_Y - 1) * Y_CAP)
+    at = [sum(sizes[:i]) for i in range(len(sizes) + 1)]
+    return [View(table, i) for i in at]
+
+
 def wait_bytes(ref, sem):
     pltpu.make_async_copy(ref, ref, sem).wait()
 
 
 def gather_kernel(
     n_tm, n_pair, own, rows,
-    slot_ref, local_ref, pick_ref, coef_ref, ener_ref,
+    table_ref, coef_ref, ener_ref,
     a_out, g_out, e_out,
     *scratch,
 ):
+    slot_ref, local_ref, pick_ref = views(table_ref, n_tm * own, n_pair)[:3]
     my_tm, my_pair = lax.axis_index("tm"), lax.axis_index("pair")
     sends, recvs = scratch[:CHUNKS], scratch[CHUNKS : 2 * CHUNKS]
     (e_send, e_recv, a_send, g_send, x_ener,
@@ -66,12 +83,11 @@
     def ener_copy(i):
         target = lax.rem(my_pair + i + 1, n_pair)
         return pltpu.make_async_remote_copy(
-            src_ref=e_send.at[i], dst_ref=e_recv.at[i],
+            src_ref=e_send.at[pl.ds(CAP * i, CAP)], dst_ref=e_recv.at[pl.ds(CAP * i, CAP)],
             send_sem=pair_send.at[CHUNKS], recv_sem=pair_recv.at[CHUNKS],
             device_id=(my_tm, target), device_id_type=MESH,
         )
 
-    row_id = lax.broadcasted_iota(jnp.int32, (16, ener_ref.shape[2]), 0)
 
     def stage_a(u):
         owner = lax.rem(my_tm + u + 1, n_tm)
@@ -90,16 +106,15 @@
         for j in range(CAP):
             recvs[c][CAP * peers + j] = coef_ref[pick_ref[CAP * peers + j], pl.ds(c * step, step), :]
 
-    def stage_ener(i):
-        tile = jnp.zeros(row_id.shape, jnp.float32)
+    def send_ener(i, carry):
         for j in range(CAP):
-            tile = jnp.where(row_id == j, ener_ref[pick_ref[CAP * i + j]].astype(jnp.float32), tile)
-        return tile.astype(jnp.bfloat16)
-
-    def send_ener(i, carry):
-        e_send[i] = stage_ener(i)
+            e_send[CAP * i + j] = ener_ref[pick_ref[CAP * i + j]]
         ener_copy(i).start()
         return carry
+
+    def keep_ener():
+        for j in range(CAP * peers, CAP * n_pair):
+            e_recv[j] = ener_ref[pick_ref[j]]
 
     def a_one(u, carry):
         owner = stage_a(u)
@@ -116,7 +131,7 @@
     own_a = pltpu.make_async_copy(a_send.at[others], a_out.at[my_tm], own_sems.at[0])
     own_a.start()
     lax.fori_loop(0, peers, send_ener, 0)
-    e_recv[peers] = stage_ener(peers)
+    keep_ener()
     for c in range(1, CHUNKS):
         send_pair(c)
 
@@ -145,19 +160,13 @@
         copy.start()
         owned_g.append(copy)
         if c == 0:
-            wait_bytes(e_recv.at[pl.ds(0, peers)], pair_recv.at[CHUNKS])
+            wait_bytes(e_recv.at[pl.ds(0, CAP * peers)], pair_recv.at[CHUNKS])
 
             def stage_x(u):
                 owner = lax.rem(my_tm + u + 1, n_tm)
-                tile = jnp.zeros(row_id.shape, jnp.float32)
                 for e in range(own):
-                    slot = slot_ref[owner * own + e]
-                    held = e_recv[slot // CAP].astype(jnp.float32)
-                    picked = jnp.sum(jnp.where(row_id == lax.rem(slot, CAP), held, 0.0), axis=0, keepdims=True)
-                    tile = jnp.where(row_id == e, picked, tile)
-                    mine = ener_ref[local_ref[owner * own + e]].astype(jnp.float32)
-                    tile = jnp.where(row_id == own + e, mine, tile)
-                x_ener[u] = tile.astype(jnp.bfloat16)
+                    x_ener[u, e] = e_recv[slot_ref[owner * own + e]]
+                    x_ener[u, own + e] = ener_ref[local_ref[owner * own + e]]
                 return owner
 
             def x_one(u, carry):
@@ -176,7 +185,7 @@
 
     for c in range(CHUNKS):
         wait_bytes(sends[c].at[pl.ds(0, CAP * peers)], pair_send.at[c])
-    wait_bytes(e_send.at[pl.ds(0, peers)], pair_send.at[CHUNKS])
+    wait_bytes(e_send.at[pl.ds(0, CAP * peers)], pair_send.at[CHUNKS])
     for side in range(2):
         wait_bytes(a_send.at[pl.ds(0, others)], a_sems.at[side])
         wait_bytes(x_ener.at[pl.ds(0, others)], e_sems.at[side])
@@ -190,66 +199,67 @@
 
 def fast_kernel(
     n_tm, n_pair, own, rows,
-    final_ref, slot_ref, local_ref, pick_ref, y_ref, z_ref, coef_ref, ener_ref,
+    table_ref, coef_ref, ener_ref,
     a_out, g_out, e_out,
     y_send, y_recv, z_send, z_recv, e_send, e_recv, x_send, x_ener, *rest,
 ):
+    slot_ref, local_ref, pick_ref, final_ref, y_ref, z_ref = views(table_ref, n_tm * own, n_pair)
     pools = rest[:POOLS]
     (y_ssem, y_rsem, z_ssem, z_rsem, pair_send, pair_recv, a_sems, g_sems, e_sems, own_sems) = rest[POOLS:]
     my_tm, my_pair = lax.axis_index("tm"), lax.axis_index("pair")
     peers, others = n_pair - 1, n_tm - 1
     n_z = n_pair // N_Y
     my_y, my_z = my_pair // n_z, lax.rem(my_pair, n_z)
-    step = rows // FAST_CHUNKS
+    assert sum(PARTS) == rows
+    spans = [pl.ds(sum(PARTS[:c]), PARTS[c]) for c in range(FAST_CHUNKS)]
     blocks = coef_ref.shape[0]
     y_slots = (N_Y - 1) * Y_CAP
     ahead = (my_y * n_z + lax.rem(my_z + 1, n_z), my_y * n_z + lax.rem(my_z + n_z - 1, n_z))
     firsts = [sum(Z_CAPS[:r]) for r in range(len(Z_CAPS) + 1)]
     greet(n_tm, n_pair, my_tm, my_pair)
-    row_id = lax.broadcasted_iota(jnp.int32, (16, ener_ref.shape[2]), 0)
 
     def ener_copy(i):
         target = lax.rem(my_pair + i + 1, n_pair)
         return pltpu.make_async_remote_copy(
-            src_ref=e_send.at[i], dst_ref=e_recv.at[i],
+            src_ref=e_send.at[pl.ds(CAP * i, CAP)], dst_ref=e_recv.at[pl.ds(CAP * i, CAP)],
             send_sem=pair_send, recv_sem=pair_recv,
             device_id=(my_tm, target), device_id_type=MESH,
         )
 
-    def stage_ener(i):
-        tile = jnp.zeros(row_id.shape, jnp.float32)
+    def send_ener(i, carry):
         for j in range(CAP):
-            tile = jnp.where(row_id == j, ener_ref[pick_ref[CAP * i + j]].astype(jnp.float32), tile)
-        return tile.astype(jnp.bfloat16)
-
-    def send_ener(i, carry):
-        e_send[i] = stage_ener(i)
+            e_send[CAP * i + j] = ener_ref[pick_ref[CAP * i + j]]
         ener_copy(i).start()
         return carry
+
+    def keep_ener():
+        for j in range(CAP * peers, CAP * n_pair):
+            e_recv[j] = ener_ref[pick_ref[j]]
 
     def send_y(c):
         for i in range(N_Y - 1):
             def one(j, carry):
-                y_send[c, i, j] = coef_ref[y_ref[i * Y_CAP + j], pl.ds(c * step, step), :]
+                y_send[i, j, spans[c]] = coef_ref[y_ref[i * Y_CAP + j], spans[c], :]
                 return carry
 
             lax.fori_loop(0, Y_CAP, one, 0)
             target = lax.rem(my_y + i + 1, N_Y) * n_z + my_z
             pltpu.make_async_remote_copy(
-                src_ref=y_send.at[c, i], dst_ref=y_recv.at[c, i],
+                src_ref=y_send.at[i, :, spans[c]], dst_ref=y_recv.at[i, :, spans[c]],
                 send_sem=y_ssem, recv_sem=y_rsem.at[c],
                 device_id=(my_tm, target), device_id_type=MESH,
             ).start()
 
     def fill(c):
         pool = pools[c % POOLS]
-        pool[pl.ds(0, blocks)] = coef_ref[:, pl.ds(c * step, step), :]
-        wait_bytes(y_recv.at[c], y_rsem.at[c])
+        held = pl.ds(0, PARTS[c])
+        pool[pl.ds(0, blocks), held] = coef_ref[:, spans[c], :]
+        wait_bytes(y_recv.at[:, :, spans[c]], y_rsem.at[c])
         for i in range(N_Y - 1):
-            pool[pl.ds(blocks + i * Y_CAP, Y_CAP)] = y_recv[c, i]
+            pool[pl.ds(blocks + i * Y_CAP, Y_CAP), held] = y_recv[i, :, spans[c]]
 
     def span(c, r, way):
-        return (c, way, pl.ds(firsts[r], Z_CAPS[r]))
+        return (way, pl.ds(firsts[r], Z_CAPS[r]), spans[c])
 
     def send_z(c, r):
         pool = pools[c % POOLS]
@@ -257,7 +267,7 @@
             base = (2 * r + way) * Z_CAPS[0]
 
             def one(j, carry):
-                z_send[c, way, firsts[r] + j] = pool[z_ref[base + j]]
+                z_send[way, firsts[r] + j, spans[c]] = pool[z_ref[base + j], pl.ds(0, PARTS[c])]
                 return carry
 
             lax.fori_loop(0, Z_CAPS[r], one, 0)
@@ -272,7 +282,7 @@
         for way in range(2):
             wait_bytes(z_recv.at[span(c, r, way)], z_rsem.at[c, r, way])
             at = blocks + y_slots + way * firsts[-1] + firsts[r]
-            pool[pl.ds(at, Z_CAPS[r])] = z_recv[span(c, r, way)]
+            pool[pl.ds(at, Z_CAPS[r]), pl.ds(0, PARTS[c])] = z_recv[span(c, r, way)]
 
     def stage_a(u):
         owner = lax.rem(my_tm + u + 1, n_tm)
@@ -291,12 +301,12 @@
 
     def send_x(c):
         pool = pools[c % POOLS]
-        part = pl.ds(c * step, step)
+        part = spans[c]
 
         def stage_g(u):
             owner = lax.rem(my_tm + u + 1, n_tm)
             for e in range(own):
-                x_send[u, e, part] = pool[final_ref[owner * own + e]]
+                x_send[u, e, part] = pool[final_ref[owner * own + e], pl.ds(0, PARTS[c])]
             return owner
 
         def g_one(u, carry):
@@ -313,19 +323,13 @@
         pltpu.make_async_copy(x_send.at[others, :, part], g_out.at[my_tm, :, part], own_sems.at[1 + c]).start()
 
     def send_x_ener():
-        wait_bytes(e_recv.at[pl.ds(0, peers)], pair_recv)
+        wait_bytes(e_recv.at[pl.ds(0, CAP * peers)], pair_recv)
 
         def stage_x(u):
             owner = lax.rem(my_tm + u + 1, n_tm)
-            tile = jnp.zeros(row_id.shape, jnp.float32)
             for e in range(own):
-                slot = slot_ref[owner * own + e]
-                held = e_recv[slot // CAP].astype(jnp.float32)
-                picked = jnp.sum(jnp.where(row_id == lax.rem(slot, CAP), held, 0.0), axis=0, keepdims=True)
-                tile = jnp.where(row_id == e, picked, tile)
-                mine = ener_ref[local_ref[owner * own + e]].astype(jnp.float32)
-                tile = jnp.where(row_id == own + e, mine, tile)
-            x_ener[u] = tile.astype(jnp.bfloat16)
+                x_ener[u, e] = e_recv[slot_ref[owner * own + e]]
+                x_ener[u, own + e] = ener_ref[local_ref[owner * own + e]]
             return owner
 
         def x_one(u, carry):
@@ -343,7 +347,7 @@
 
     send_y(0)
     lax.fori_loop(0, peers, send_ener, 0)
-    e_recv[peers] = stage_ener(peers)
+    keep_ener()
     send_y(1)
     lax.fori_loop(0, others, a_one, 0)
     stage_a(others)
@@ -384,120 +388,88 @@
 
     wait_bytes(y_send, y_ssem)
     wait_bytes(z_send, z_ssem)
-    wait_bytes(e_send.at[pl.ds(0, peers)], pair_send)
+    wait_bytes(e_send.at[pl.ds(0, CAP * peers)], pair_send)
     wait_bytes(x_send.at[pl.ds(0, others)], a_sems.at[1])
     for side in range(2):
         wait_bytes(x_ener.at[pl.ds(0, others)], e_sems.at[side])
         for c in range(FAST_CHUNKS):
-            wait_bytes(x_send.at[pl.ds(0, others), :, pl.ds(c * step, step)], g_sems.at[side, c])
+            wait_bytes(x_send.at[pl.ds(0, others), :, spans[c]], g_sems.at[side, c])
     for c in range(FAST_CHUNKS):
-        part = pl.ds(c * step, step)
+        part = spans[c]
         pltpu.make_async_copy(x_send.at[others, :, part], g_out.at[my_tm, :, part], own_sems.at[1 + c]).wait()
     pltpu.make_async_copy(x_ener.at[others], e_out.at[my_tm], own_sems.at[1 + FAST_CHUNKS]).wait()
-
-
-def list_fits(n_pair, live, source):
-    n_z = n_pair // N_Y
-    ids = jnp.arange(n_pair, dtype=jnp.int32)
-    count = jnp.sum((source[:, :, None] == ids).astype(jnp.int32), axis=1)
-    by_y = jnp.sum(count.reshape(N_Y, n_z, N_Y, n_z), axis=1)
-    far = jnp.arange(N_Y)[:, None, None] != jnp.arange(N_Y)[None, :, None]
-    fits = jnp.all(jnp.where(far, by_y, 0) <= Y_CAP)
-    at = jnp.sum(count.reshape(N_Y, n_z, N_Y, n_z), axis=2)
-    half = n_z // 2
-    y_id, z_id = jnp.arange(N_Y)[:, None], jnp.arange(n_z)[None, :]
-    zd_id, zs_id = jnp.arange(n_z)[:, None], jnp.arange(n_z)[None, :]
-    delta = (zd_id - zs_id) % n_z
-    for way in range(2):
-        queue = [None]
-        for far_by in range(1, half + 1):
-            gap = far_by if way == 0 else n_z - far_by
-            n = jnp.sum(jnp.where(delta[None] == gap, at, 0), axis=1)
-            if far_by == half:
-                even = (y_id + z_id) % 2 == 0
-                n = (n + jnp.where(even, 1 - way, way)) // 2
-            queue.append(n)
-        for cap in Z_CAPS:
-            left = jnp.full((N_Y, n_z), cap, jnp.int32)
-            moved = [None] * (half + 1)
-            for far_by in range(half, 0, -1):
-                moved[far_by] = jnp.minimum(queue[far_by], left)
-                left = left - moved[far_by]
-            for far_by in range(1, half + 1):
-                queue[far_by] = queue[far_by] - moved[far_by]
-                if far_by < half:
-                    queue[far_by] = queue[far_by] + jnp.roll(moved[far_by + 1], 1 - 2 * way, axis=1)
-        fits = fits & (sum(jnp.sum(q) for q in queue[1:]) == 0)
-    return fits
 
 
 def routes(n_pair, blocks, my_pair, live, source, held, rank):
     listed = live.shape[1]
     n_z = n_pair // N_Y
+    n = n_z * listed
     my_y, my_z = my_pair // n_z, my_pair % n_z
     rows = jnp.arange(n_pair, dtype=jnp.int32)
     mine = source == my_pair
     per_row = jnp.sum(mine.astype(jnp.int32), axis=1)
     same = (rows[:, None] // n_z == rows[None, :] // n_z) & (rows[None, :] < rows[:, None])
     first = jnp.sum(jnp.where(same, per_row[None, :], 0), axis=1)
-    place = jnp.where(mine, first[:, None] + rank, -1).reshape(N_Y, 1, n_z * listed)
+    place = jnp.where(mine, first[:, None] + rank, -1).reshape(N_Y, 1, n)
     want = jnp.arange(Y_CAP, dtype=jnp.int32)[None, :, None]
-    y_tab = jnp.sum(jnp.where(place == want, held.reshape(N_Y, 1, n_z * listed), 0), axis=2)
+    y_tab = jnp.sum(jnp.where(place == want, held.reshape(N_Y, 1, n), 0), axis=2)
     y_tab = lax.dynamic_slice_in_dim(jnp.concatenate([y_tab, y_tab]), my_y + 1, N_Y - 1)
-
-    ring = lambda v: lax.dynamic_slice_in_dim(v, my_y * n_z, n_z).reshape(n_z * listed)
-    src, hold, alive = ring(source), ring(held), ring(live)
-    n = n_z * listed
+    ring_source = source.reshape(N_Y, n)
+    count = jnp.sum((ring_source[:, None, :] == rows[None, :, None]).astype(jnp.int32), axis=2)
+    leg = jnp.where(rows[None, :] // n_z == jnp.arange(N_Y)[:, None], 0, count)
+
+    pos_in = jnp.arange(listed, dtype=jnp.int32)
+    z_key = jnp.where(live, source % n_z, -1)
+    z_same = (z_key[:, :, None] == z_key[:, None, :]) & (pos_in[None, :] < pos_in[:, None])[None]
+    z_rank = jnp.sum(z_same.astype(jnp.int32), axis=2).reshape(N_Y, n)
     ids = jnp.arange(n, dtype=jnp.int32)
     zd = ids // listed
-    ys, zs = src // n_z, src % n_z
+    zs = ring_source % n_z
+    delta = (zd[None, :] - zs) % n_z
+    half = n_z // 2
+    plus = (delta < half) | ((delta == half) & ((z_rank + zs + jnp.arange(N_Y)[:, None]) % 2 == 0))
+    way = jnp.where(plus, 0, 1)
+    rem = jnp.where(live.reshape(N_Y, n), jnp.where(plus, delta, n_z - delta), 0)
+    pos = zs
+
+    ring = lambda v: lax.dynamic_index_in_dim(v, my_y, 0, keepdims=False)
+    src, my_way = ring(ring_source), ring(way)
     earlier = ids[None, :] < ids[:, None]
     y_rank = jnp.sum(((src[:, None] == src[None, :]) & earlier).astype(jnp.int32), axis=1)
-    z_key = jnp.where(alive, zs, -1)
-    z_rank = jnp.sum(
-        ((z_key[:, None] == z_key[None, :]) & (zd[:, None] == zd[None, :]) & earlier).astype(jnp.int32), axis=1
-    )
-    step_y = (my_y - ys) % N_Y
-    loc = jnp.where(step_y == 0, hold, blocks + (step_y - 1) * Y_CAP + y_rank)
-    loc = jnp.where(alive, loc, 0)
-    delta = (zd - zs) % n_z
-    half = n_z // 2
-    plus = (delta < half) | ((delta == half) & ((z_rank + zs + my_y) % 2 == 0))
-    way = jnp.where(plus, 0, 1)
-    rem = jnp.where(alive, jnp.where(plus, delta, n_z - delta), 0)
-    pos = zs
+    step_y = (my_y - src // n_z) % N_Y
+    loc = jnp.where(step_y == 0, ring(held.reshape(N_Y, n)), blocks + (step_y - 1) * Y_CAP + y_rank)
+    loc = jnp.where(src >= 0, loc, 0)
     total = sum(Z_CAPS)
     tables, begun = [], 0
     slots = jnp.arange(Z_CAPS[0], dtype=jnp.int32)
     for cap in Z_CAPS:
-        active = rem > 0
-        group = jnp.where(active, pos * 2 + way, -1)
-        key = rem * n - ids
-        ahead = (group[:, None] == group[None, :]) & (key[None, :] > key[:, None])
-        order = jnp.sum(ahead.astype(jnp.int32), axis=1)
-        moved = active & (order < cap)
+        group = jnp.where(rem > 0, pos * 2 + way, -1)
+        key = rem * n - ids[None, :]
+        ahead = (group[:, :, None] == group[:, None, :]) & (key[:, None, :] > key[:, :, None])
+        order = jnp.sum(ahead.astype(jnp.int32), axis=2)
+        moved = (rem > 0) & (order < cap)
+        my_order, my_moved, my_group = ring(order), ring(moved), ring(group)
         for w in range(2):
-            here = jnp.where(moved & (group == my_z * 2 + w), order, -1)
+            here = jnp.where(my_moved & (my_group == my_z * 2 + w), my_order, -1)
             tables.append(jnp.sum(jnp.where(here[None, :] == slots[:, None], loc[None, :], 0), axis=1))
-        to = blocks + (N_Y - 1) * Y_CAP + way * total + begun + order
-        loc = jnp.where(moved, to, loc)
+        loc = jnp.where(my_moved, blocks + (N_Y - 1) * Y_CAP + my_way * total + begun + my_order, loc)
         pos = jnp.where(moved, (pos + jnp.where(plus, 1, n_z - 1)) % n_z, pos)
         rem = rem - moved.astype(jnp.int32)
         begun += cap
     final = lax.dynamic_slice_in_dim(loc, my_z * listed, listed)
-    return y_tab.reshape(-1), jnp.concatenate(tables), final
+    fits = jnp.maximum(jnp.max(rem), jnp.max(leg - Y_CAP)) <= 0
+    return fits, y_tab.reshape(-1), jnp.concatenate(tables), final
 
 
 def entry_kernel(own, n_time, a_ref, g_ref, e_ref, tile_ref, cos_ref, tau_ref, live_ref, w_ref, c_ref, x_ref, y_ref):
     e = pl.program_id(0)
     slices, _, size, width = a_ref.shape
     live = live_ref[e]
-    row_id = lax.broadcasted_iota(jnp.int32, (16, width), 0)
+    lines = lambda v: jnp.concatenate([v[i : i + 1] for i in range(v.shape[0])], axis=1)
     chi = [jnp.zeros((size, size), jnp.float32) for _ in range(n_time)]
     for m in range(slices):
-        ener = e_ref[m].astype(jnp.float32)
-        eg = jnp.sum(jnp.where(row_id == e, ener, 0.0), axis=0, keepdims=True)
-        ea = jnp.sum(jnp.where(row_id == own + e, ener, 0.0), axis=0, keepdims=True)
+        eg = lines(e_ref[m, e])
+        ea = lines(e_ref[m, own + e])
         a = a_ref[m, 0].astype(jnp.float32)
         g = g_ref[m, 0].astype(jnp.float32)
         for t in range(n_time):
@@ -532,7 +504,7 @@
 
 def return_kernel(
     n_tm, n_pair, own,
-    back_ref, keep_ref, contrib_ref, owning_ref,
+    back_ref, contrib_ref, owning_ref,
     out_ref,
     c_send, c_recv, p_send, p_recv, tm_sems, pair_sems,
 ):
@@ -540,7 +512,6 @@
     peers, others = n_pair - 1, n_tm - 1
     width = out_ref.shape[1]
     c_send[...] = jnp.zeros_like(c_send)
-    p_send[...] = jnp.zeros_like(p_send)
     greet(n_tm, n_pair, my_tm, my_pair)
 
     def stage_c(u):
@@ -566,14 +537,17 @@
     def stage_p(i):
         for j in range(CAP):
             at = back_ref[CAP * i + j]
-            keep = keep_ref[CAP * i + j]
-            p_send[i, pl.ds(j, 1), :] = c_recv[at // own, pl.ds(lax.rem(at, own), 1), :] * keep
+            keep = jnp.where(at >= 0, 1.0, 0.0)
+            at = jnp.maximum(at, 0)
+            line = c_recv[at // own, pl.ds(lax.rem(at, own), 1), :] * keep
+            for h in range(width // LINE):
+                p_send[CAP * i + j, pl.ds(h, 1), :] = line[:, h * LINE : (h + 1) * LINE]
 
     def pair_one(i, carry):
         stage_p(i)
         target = lax.rem(my_pair + n_pair - 1 - i, n_pair)
         pltpu.make_async_remote_copy(
-            src_ref=p_send.at[i], dst_ref=p_recv.at[i],
+            src_ref=p_send.at[pl.ds(CAP * i, CAP)], dst_ref=p_recv.at[pl.ds(CAP * i, CAP)],
             send_sem=pair_sems.at[0], recv_sem=pair_sems.at[1],
             device_id=(my_tm, target), device_id_type=MESH,
         ).start()
@@ -581,14 +555,15 @@
 
     lax.fori_loop(0, peers, pair_one, 0)
     stage_p(peers)
-    wait_bytes(p_recv.at[pl.ds(0, peers)], pair_sems.at[1])
-    p_recv[peers] = p_send[peers]
-    incoming = p_recv[...].reshape(n_pair * 8, width)
-    out_ref[...] = jnp.dot(
-        owning_ref[...], incoming, precision=lax.Precision.HIGHEST, preferred_element_type=jnp.float32
-    )
+    wait_bytes(p_recv.at[pl.ds(0, CAP * peers)], pair_sems.at[1])
+    for j in range(CAP * peers, CAP * n_pair):
+        p_recv[j] = p_send[j]
+    for h in range(width // LINE):
+        out_ref[:, pl.ds(h * LINE, LINE)] = jnp.dot(
+            owning_ref[...], p_recv[:, h, :], precision=lax.Precision.HIGHEST, preferred_element_type=jnp.float32
+        )
     wait_bytes(c_send.at[pl.ds(0, others)], tm_sems.at[0])
-    wait_bytes(p_send.at[pl.ds(0, peers)], pair_sems.at[0])
+    wait_bytes(p_send.at[pl.ds(0, CAP * peers)], pair_sems.at[0])
 
 
 def body(n_tm, n_pair, coefs, energies, coulomb, tau_grid, freq_grid, pairs):
@@ -618,14 +593,13 @@
     lane = jnp.arange(n_pair * CAP, dtype=jnp.int32)
     match = (slot[None, :] == lane[:, None]) & my_live[None, :]
     back = jnp.sum(jnp.where(match, pos[None, :], 0), axis=1)
-    back_keep = jnp.sum(match.astype(jnp.float32), axis=1)
     back = ((my_tm - back // own + n_tm - 1) % n_tm) * own + back % own
-    tall = jnp.arange(8, dtype=jnp.int32)
-    pick8 = jnp.pad(jnp.where(used > 0, pick, -1), ((0, 0), (0, 8 - CAP)), constant_values=-1)
-    owning = (jnp.arange(blocks, dtype=jnp.int32)[:, None] == pick8.reshape(1, -1)).astype(jnp.float32)
+    back = jnp.where(jnp.any(match, axis=1), back, -1)
+    given = jnp.where(used > 0, pick, -1).reshape(1, -1)
+    owning = (jnp.arange(blocks, dtype=jnp.int32)[:, None] == given).astype(jnp.float32)
     my_owned = lax.dynamic_slice_in_dim(my_live, my_tm * own, own).astype(jnp.float32)
     cosine = jnp.cos(freq_grid[:, None] * tau_grid[None, :])
-    ener16 = jnp.broadcast_to(energies[:, None, :], (blocks, 16, width))
+    lined = energies.astype(jnp.float32).reshape(blocks, width // LINE, LINE)
 
     smem = pl.BlockSpec(memory_space=pltpu.SMEM)
     vmem = pl.BlockSpec(memory_space=pltpu.VMEM)
@@ -637,29 +611,28 @@
     gathered = (
         jax.ShapeDtypeStruct((n_tm, own, size, width), bf16),
         jax.ShapeDtypeStruct((n_tm, own, size, width), bf16),
-        jax.ShapeDtypeStruct((n_tm, 16, width), bf16),
+        jax.ShapeDtypeStruct((n_tm, 2 * own, width // LINE, LINE), jnp.float32),
     )
-    fits = list_fits(n_pair, live, source)
-    y_tab, z_tab, final = routes(n_pair, blocks, my_pair, live, source, held, rank)
-    pick_flat = pick.reshape(-1)
-
-    def pooled(slot, my_local, pick_flat, y_tab, z_tab, final, coefs, ener16):
+    fits, y_tab, z_tab, final = routes(n_pair, blocks, my_pair, live, source, held, rank)
+    table = jnp.concatenate([slot, my_local, pick.reshape(-1), final, y_tab, z_tab]).astype(jnp.int32)
+
+    def pooled(table, coefs, lined):
         total = sum(Z_CAPS)
         depth = blocks + (N_Y - 1) * Y_CAP + 2 * total
         return pl.pallas_call(
             functools.partial(fast_kernel, n_tm, n_pair, own, size),
             out_shape=gathered,
-            in_specs=[smem] * 6 + [vmem] * 2,
+            in_specs=[smem] + [vmem] * 2,
             out_specs=(hbm, hbm, hbm),
-            scratch_shapes=[pltpu.VMEM((FAST_CHUNKS, N_Y - 1, Y_CAP, thin, width), bf16)] * 2
-            + [pltpu.VMEM((FAST_CHUNKS, 2, total, thin, width), bf16)] * 2
+            scratch_shapes=[pltpu.VMEM((N_Y - 1, Y_CAP, size, width), bf16)] * 2
+            + [pltpu.VMEM((2, total, size, width), bf16)] * 2
             + [
-                pltpu.VMEM((n_pair, 16, width), bf16),
-                pltpu.VMEM((n_pair, 16, width), bf16),
+                pltpu.VMEM((CAP * n_pair, width // LINE, LINE), jnp.float32),
+                pltpu.VMEM((CAP * n_pair, width // LINE, LINE), jnp.float32),
                 pltpu.VMEM((n_tm, own, size, width), bf16),
-                pltpu.VMEM((n_tm, 16, width), bf16),
+                pltpu.VMEM((n_tm, 2 * own, width // LINE, LINE), jnp.float32),
             ]
-            + [pltpu.VMEM((depth, thin, width), bf16)] * POOLS
+            + [pltpu.VMEM((depth, max(PARTS), width), bf16)] * POOLS
             + [
                 DMA,
                 DMA((FAST_CHUNKS,)),
@@ -675,21 +648,21 @@
             compiler_params=pltpu.CompilerParams(
                 collective_id=2, has_side_effects=True, vmem_limit_bytes=62 * 1024 * 1024
             ),
-        )(final, slot, my_local, pick_flat, y_tab, z_tab, coefs, ener16)
-
-    def direct(slot, my_local, pick_flat, y_tab, z_tab, final, coefs, ener16):
+        )(table, coefs, lined)
+
+    def direct(table, coefs, lined):
         return pl.pallas_call(
             functools.partial(gather_kernel, n_tm, n_pair, own, size),
             out_shape=gathered,
-            in_specs=[smem] * 3 + [vmem] * 2,
+            in_specs=[smem] + [vmem] * 2,
             out_specs=(hbm, hbm, hbm),
             scratch_shapes=[pltpu.VMEM((CAP * n_pair, step, width), bf16)] * (2 * CHUNKS)
             + [
-                pltpu.VMEM((n_pair, 16, width), bf16),
-                pltpu.VMEM((n_pair, 16, width), bf16),
+                pltpu.VMEM((CAP * n_pair, width // LINE, LINE), jnp.float32),
+                pltpu.VMEM((CAP * n_pair, width // LINE, LINE), jnp.float32),
                 pltpu.VMEM((n_tm, own, size, width), bf16),
                 pltpu.VMEM((CHUNKS, n_tm, own, step, width), bf16),
-                pltpu.VMEM((n_tm, 16, width), bf16),
+                pltpu.VMEM((n_tm, 2 * own, width // LINE, LINE), jnp.float32),
                 DMA((CHUNKS + 1,)),
                 DMA((CHUNKS + 1,)),
                 DMA((2,)),
@@ -700,10 +673,10 @@
             compiler_params=pltpu.CompilerParams(
                 collective_id=0, has_side_effects=True, vmem_limit_bytes=56 * 1024 * 1024
             ),
-        )(slot, my_local, pick_flat, coefs, ener16)
+        )(table, coefs, lined)
 
     a_all, g_all, e_all = lax.cond(
-        fits, pooled, direct, slot, my_local, pick_flat, y_tab, z_tab, final, coefs, ener16
+        fits, pooled, direct, table, coefs, lined
     )
 
     screened, contrib = pl.pallas_call(
@@ -716,7 +689,7 @@
         in_specs=[
             pl.BlockSpec((n_tm, 1, size, width), lambda e: (0, e, 0, 0)),
             pl.BlockSpec((n_tm, 1, size, width), lambda e: (0, e, 0, 0)),
-            pl.BlockSpec((n_tm, 16, width), lambda e: (0, 0, 0)),
+            pl.BlockSpec((n_tm, 2 * own, width // LINE, LINE), lambda e: (0, 0, 0, 0)),
             pl.BlockSpec((1, size, size), lambda e: (e, 0, 0)),
             smem, smem, smem,
         ],
@@ -731,18 +704,18 @@
     self_energy = pl.pallas_call(
         functools.partial(return_kernel, n_tm, n_pair, own),
         out_shape=jax.ShapeDtypeStruct((blocks, width), jnp.float32),
-        in_specs=[smem, smem, vmem, vmem],
+        in_specs=[smem, vmem, vmem],
         out_specs=vmem,
         scratch_shapes=[
             pltpu.VMEM((n_tm, 8, width), jnp.float32),
             pltpu.VMEM((n_tm, 8, width), jnp.float32),
-            pltpu.VMEM((n_pair, 8, width), jnp.float32),
-            pltpu.VMEM((n_pair, 8, width), jnp.float32),
+            pltpu.VMEM((CAP * n_pair, width // LINE, LINE), jnp.float32),
+            pltpu.VMEM((CAP * n_pair, width // LINE, LINE), jnp.float32),
             DMA((2,)),
             DMA((2,)),
         ],
         compiler_params=pltpu.CompilerParams(collective_id=1, has_side_effects=True),
-    )(back, back_keep, contrib, owning)
+    )(back, contrib, owning)
     return (screened[None], self_energy)
 
 

time: 225 us -> 213 us (0.947)
  between operations: 6.7 us -> 2.2 us
  Pallas kernels: 198 us -> 195 us
  local copies, waits for them, and re-layouts: 8.04 us -> 5.47 us
  other arithmetic: 11.8 us -> 9.42 us
    pallas_call x1, Pallas kernels: 18.4 us -> 13.7 us  [body(): pl.pallas_call(functools.partial(return_kernel, n_tm, n_pair, own), out_s...]
    reduce_sum x15 -> x6, other arithmetic: 6.64 us -> 2.58 us  [the longest x4 2.09 us: routes(): order = jnp.sum(ahead.astype(jnp.int32), axis=2)]
    pallas_call x1, Pallas kernels: 165 us -> 167 us  [pooled(): pl.pallas_call(functools.partial(fast_kernel, n_tm, n_pair, own, size), o...]
where the time goes in v3:
time: 213 us
  Pallas kernels  195 us (92%)
  other arithmetic  9.42 us (4%)
  local copies, waits for them, and re-layouts  5.47 us (3%)
  between operations  2.2 us (1%)
    pallas_call x1, Pallas kernels, pooled(): pl.pallas_call(functools.partial(fast_kernel, n_tm, n_pair, own, size), o...  167 us
    pallas_call x1, Pallas kernels, body(): pl.pallas_call(functools.partial(entry_kernel, own, n_time), grid=(own,),...  14.7 us
    pallas_call x1, Pallas kernels, body(): pl.pallas_call(functools.partial(return_kernel, n_tm, n_pair, own), out_s...  13.7 us

profile of v3, /device:TPU:1, one launch (start us, length us, event | category | flops | bytes accessed | tf_op | source)
XLA Modules:
  0.0 212.6 jit_solution(10592040214817681918)
XLA Ops:
  0.7 0.8 multiply_cosine_fusion.cos_ref
  1.5 0.1 add.815
  1.6 0.9 fusion.87
  2.4 0.1 squeeze.52
  2.6 0.1 convert_reduce_fusion.9
  2.7 0.1 fusion.57.live_ref
  2.8 1.4 convert_reduce_fusion.4
  4.2 0.1 convert_reduce_fusion.8
  4.4 0.2 select_reduce_fusion.11
  4.8 0.1 select_reduce_fusion.2
  4.9 0.1 fusion.17
  5.0 0.5 fusion.53.back_ref
  5.5 0.1 add.865
  5.8 0.1 add.867
  6.0 0.2 convert_reduce_fusion.6
  6.2 0.1 convert_reduce_fusion.7
  6.3 0.6 add_reduce_fusion
  7.0 0.3 select_reduce_fusion
  7.3 0.1 dynamic-slice_add_fusion
  7.4 0.1 copy.14
  7.5 0.1 reshape.1250
  7.6 0.5 convert_reduce_fusion.3
  8.2 0.1 lt.375
  8.3 0.5 convert_reduce_fusion.2
  8.9 0.1 lt.378
  9.0 0.5 convert_reduce_fusion.1
  9.6 0.5 convert_reduce_fusion
  10.2 0.1 select_reduce_fusion.5
  10.4 0.1 select_reduce_fusion.3
  10.5 0.1 dynamic_slice.93
  10.6 0.1 select_reduce_fusion.7
  10.7 0.1 select_reduce_fusion.9
  10.8 0.1 lt.385
  10.9 0.1 lt.381
  11.0 0.7 subtract_reduce_fusion
  13.0 0.1 copy.15
  13.1 0.1 eq.609
  13.2 0.1 copy.13
  13.3 0.1 reshape.1249
  13.4 0.1 concatenate.14
  13.5 0.6 fusion.2.owning_ref
  14.1 0.8 reshape.1254
  15.0 167.1 %conditional.1 = ((bf16[8,4,256,256]{3,2,1,0:T(8,128)(2,1)}, bf16[8,4,256,256]{3,2,1,0:T(8,128)(2,1)}, f32[8,8,2,128]{3,2,1,0:T(2,128)S(1)})) conditional(s32[]{:T(128)} %convert_element_type.155, (s32[285]{0:T(512)S(1)}, bf16[64,256,256]{2,1,0:T(8,128)(2,1)}, f32[64,2,128]{2,1,0:T(2,128)S(1)}) %tuple.14, (s32[285]{0:T(512)S(1)}, ...), branch_computations={%region_22.23_spmd, %region_23.24_spmd} | conditional | bytes 8 | solution.py:678
  15.0 166.9 %branch_1_fun.1 = (bf16[8,4,256,256]{3,2,1,0:T(8,128)(2,1)}, bf16[8,4,256,256]{3,2,1,0:T(8,128)(2,1)}, f32[8,8,2,128]{3,2,1,0:T(2,128)S(1)}) custom-call(s32[285]{0:T(512)S(1)} %get-tuple-element.15.table_ref, bf16[64,256,256]{2,1,0:T(8,128)(2,1)} %get-tuple-element.16.coef_ref, f32[64,2,128]{2,1,0:T(2,128)S(1)} %get-tuple-element.17.ener_ref), custom_call_target="tpu_custom_call" | custom-call | tf_op jit(solution)/shard_map/cond/branch_1_fun/pallas_call | solution.py:622
  182.1 14.7 %shard_map.77 = (bf16[4,3,256,256]{3,2,1,0:T(8,128)(2,1)}, f32[4,8,256]{2,1,0:T(8,128)S(1)}) custom-call(bf16[8,4,256,256]{3,2,1,0:T(8,128)(2,1)} %get-tuple-element.25.a_ref, bf16[8,4,256,256]{3,2,1,0:T(8,128)(2,1)} %get-tuple-element.26.g_ref, f32[8,8,2,128]{3,2,1,0:T(2,128)S(1)} %get-tuple-element.27.e_ref, bf16[4,256,256]{2,1,0:T(8,128)(2,1)S(1)} %bitcast.63, ...), custom_call_target="tpu_custom_call" | custom-call | tf_op jit(solution)/shard_map/pallas_call | solution.py:682
  196.8 0.6 copy-done.1
  197.4 13.7 %shard_map.78 = f32[64,256]{1,0:T(8,128)} custom-call(s32[64]{0:T(128)} %fusion.53.back_ref, f32[4,8,256]{2,1,0:T(8,128)} %copy-done.1, f32[64,64]{1,0:T(8,128)} %fusion.2.owning_ref), custom_call_target="tpu_custom_call" | custom-call | tf_op jit(solution)/shard_map/pallas_call | solution.py:704
  211.2 1.5 copy.24
  (39 shorter events, 1.0 us)
Async XLA Ops:
  14.9 167.1 %copy-start = (bf16[1,4,256,256]{3,2,1,0:T(8,128)(2,1)S(1)}, bf16[1,4,256,256]{3,2,1,0:T(8,128)(2,1)}, u32[]{:S(2)}) copy-start(bf16[1,4,256,256]{3,2,1,0:T(8,128)(2,1)} %param.10) | copy-start | bytes 1572868
  14.9 167.1 %copy-start.2 = (f32[3]{0:T(128)S(1)}, f32[3]{0:T(128)}, u32[]{:S(2)}) copy-start(f32[3]{0:T(128)} %tau_ref.1) | copy-start | bytes 40
  196.8 0.6 copy-start.1

commit v4 on v3

--- a/solution.py
+++ b/solution.py
@@ -3,6 +3,7 @@
 
 import jax
 import jax.numpy as jnp
+import numpy as np
 from jax import lax
 from jax.experimental import pallas as pl
 from jax.experimental.pallas import tpu as pltpu
@@ -13,7 +14,7 @@
 PARTS = (16, 16, 32, 32, 32, 32, 32, 32, 16, 16)
 FAST_CHUNKS = len(PARTS)
 Y_CAP = 15
-Z_CAPS = (10, 10, 10, 9)
+Z_CAPS = (10, 10, 9, 8)
 LINE = 128
 N_Y = 4
 POOLS = 3
@@ -201,7 +202,7 @@
     n_tm, n_pair, own, rows,
     table_ref, coef_ref, ener_ref,
     a_out, g_out, e_out,
-    y_send, y_recv, z_send, z_recv, e_send, e_recv, x_send, x_ener, *rest,
+    y_send, y_recv, z_send, z_recv, e_send, e_recv, a_send, x_send, x_ener, *rest,
 ):
     slot_ref, local_ref, pick_ref, final_ref, y_ref, z_ref = views(table_ref, n_tm * own, n_pair)
     pools = rest[:POOLS]
@@ -211,8 +212,10 @@
     n_z = n_pair // N_Y
     my_y, my_z = my_pair // n_z, lax.rem(my_pair, n_z)
     assert sum(PARTS) == rows
-    spans = [pl.ds(sum(PARTS[:c]), PARTS[c]) for c in range(FAST_CHUNKS)]
-    blocks = coef_ref.shape[0]
+    begin = [sum(PARTS[:c]) for c in range(FAST_CHUNKS)]
+    spans = [pl.ds(begin[c], PARTS[c]) for c in range(FAST_CHUNKS)]
+    y_rows = [pl.ds(Y_CAP * begin[c], Y_CAP * PARTS[c]) for c in range(FAST_CHUNKS)]
+    blocks, _, width = coef_ref.shape
     y_slots = (N_Y - 1) * Y_CAP
     ahead = (my_y * n_z + lax.rem(my_z + 1, n_z), my_y * n_z + lax.rem(my_z + n_z - 1, n_z))
     firsts = [sum(Z_CAPS[:r]) for r in range(len(Z_CAPS) + 1)]
@@ -239,13 +242,13 @@
     def send_y(c):
         for i in range(N_Y - 1):
             def one(j, carry):
-                y_send[i, j, spans[c]] = coef_ref[y_ref[i * Y_CAP + j], spans[c], :]
+                y_send[i, pl.ds(pl.multiple_of(Y_CAP * begin[c] + j * PARTS[c], 16), PARTS[c]), :] = coef_ref[y_ref[i * Y_CAP + j], spans[c], :]
                 return carry
 
             lax.fori_loop(0, Y_CAP, one, 0)
             target = lax.rem(my_y + i + 1, N_Y) * n_z + my_z
             pltpu.make_async_remote_copy(
-                src_ref=y_send.at[i, :, spans[c]], dst_ref=y_recv.at[i, :, spans[c]],
+                src_ref=y_send.at[i, y_rows[c]], dst_ref=y_recv.at[i, y_rows[c]],
                 send_sem=y_ssem, recv_sem=y_rsem.at[c],
                 device_id=(my_tm, target), device_id_type=MESH,
             ).start()
@@ -254,12 +257,12 @@
         pool = pools[c % POOLS]
         held = pl.ds(0, PARTS[c])
         pool[pl.ds(0, blocks), held] = coef_ref[:, spans[c], :]
-        wait_bytes(y_recv.at[:, :, spans[c]], y_rsem.at[c])
+        wait_bytes(y_recv.at[:, y_rows[c]], y_rsem.at[c])
         for i in range(N_Y - 1):
-            pool[pl.ds(blocks + i * Y_CAP, Y_CAP), held] = y_recv[i, :, spans[c]]
+            pool[pl.ds(blocks + i * Y_CAP, Y_CAP), held] = y_recv[i, y_rows[c]].reshape(Y_CAP, PARTS[c], width)
 
     def span(c, r, way):
-        return (way, pl.ds(firsts[r], Z_CAPS[r]), spans[c])
+        return (way, pl.ds(firsts[-1] * begin[c] + firsts[r] * PARTS[c], Z_CAPS[r] * PARTS[c]))
 
     def send_z(c, r):
         pool = pools[c % POOLS]
@@ -267,7 +270,8 @@
             base = (2 * r + way) * Z_CAPS[0]
 
             def one(j, carry):
-                z_send[way, firsts[r] + j, spans[c]] = pool[z_ref[base + j], pl.ds(0, PARTS[c])]
+                at = firsts[-1] * begin[c] + (firsts[r] + j) * PARTS[c]
+                z_send[way, pl.ds(pl.multiple_of(at, 16), PARTS[c]), :] = pool[z_ref[base + j], pl.ds(0, PARTS[c])]
                 return carry
 
             lax.fori_loop(0, Z_CAPS[r], one, 0)
@@ -282,18 +286,18 @@
         for way in range(2):
             wait_bytes(z_recv.at[span(c, r, way)], z_rsem.at[c, r, way])
             at = blocks + y_slots + way * firsts[-1] + firsts[r]
-            pool[pl.ds(at, Z_CAPS[r]), pl.ds(0, PARTS[c])] = z_recv[span(c, r, way)]
+            pool[pl.ds(at, Z_CAPS[r]), pl.ds(0, PARTS[c])] = z_recv[span(c, r, way)].reshape(Z_CAPS[r], PARTS[c], width)
 
     def stage_a(u):
         owner = lax.rem(my_tm + u + 1, n_tm)
         for e in range(own):
-            x_send[u, e] = coef_ref[local_ref[owner * own + e]]
+            a_send[u, e] = coef_ref[local_ref[owner * own + e]]
         return owner
 
     def a_one(u, carry):
         owner = stage_a(u)
         pltpu.make_async_remote_copy(
-            src_ref=x_send.at[u], dst_ref=a_out.at[my_tm],
+            src_ref=a_send.at[u], dst_ref=a_out.at[my_tm],
             send_sem=a_sems.at[0], recv_sem=a_sems.at[1],
             device_id=(owner, my_pair), device_id_type=MESH,
         ).start()
@@ -345,52 +349,65 @@
         stage_x(others)
         pltpu.make_async_copy(x_ener.at[others], e_out.at[my_tm], own_sems.at[1 + FAST_CHUNKS]).start()
 
+    def own_a():
+        stage_a(others)
+        pltpu.make_async_copy(a_send.at[others], a_out.at[my_tm], own_sems.at[0]).start()
+
+    tasks = [functools.partial(lax.fori_loop, u, u + 1, a_one, 0) for u in range(others)]
+    tasks.append(own_a)
+    few = 4
+    for i in range(0, peers, few):
+        tasks.append(functools.partial(lax.fori_loop, i, min(i + few, peers), send_ener, 0))
+    tasks.append(keep_ener)
+
+    def spare():
+        if tasks:
+            tasks.pop(0)()
+
+    last = len(Z_CAPS) - 1
+    sent_ener = False
     send_y(0)
-    lax.fori_loop(0, peers, send_ener, 0)
-    keep_ener()
     send_y(1)
-    lax.fori_loop(0, others, a_one, 0)
-    stage_a(others)
-    own_a = pltpu.make_async_copy(x_send.at[others], a_out.at[my_tm], own_sems.at[0])
-    own_a.start()
-    last = len(Z_CAPS) - 1
     fill(0)
     send_z(0, 0)
+    send_y(2)
     fill(1)
     send_z(1, 0)
+    send_y(3)
+    spare()
     for first in range(0, FAST_CHUNKS, 2):
         second = first + 1
         more = first + 2 < FAST_CHUNKS
-        if more:
-            send_y(first + 2)
         for r in range(last):
             take_z(first, r)
             send_z(first, r + 1)
+            spare()
             take_z(second, r)
             send_z(second, r + 1)
-            if more and r == 0:
-                send_y(first + 3)
+            spare()
+            if first + 4 + r < FAST_CHUNKS and r < 2:
+                send_y(first + 4 + r)
         if more:
             fill(first + 2)
             send_z(first + 2, 0)
         take_z(first, last)
-        if first == 0:
-            own_a.wait()
-            wait_bytes(x_send.at[pl.ds(0, others)], a_sems.at[0])
         send_x(first)
         if more:
             fill(first + 3)
             send_z(first + 3, 0)
         take_z(second, last)
         send_x(second)
-        if first == 0:
+        if not tasks and not sent_ener:
+            sent_ener = True
             send_x_ener()
+    assert sent_ener
 
     wait_bytes(y_send, y_ssem)
     wait_bytes(z_send, z_ssem)
     wait_bytes(e_send.at[pl.ds(0, CAP * peers)], pair_send)
-    wait_bytes(x_send.at[pl.ds(0, others)], a_sems.at[1])
+    pltpu.make_async_copy(a_send.at[others], a_out.at[my_tm], own_sems.at[0]).wait()
     for side in range(2):
+        wait_bytes(a_send.at[pl.ds(0, others)], a_sems.at[side])
         wait_bytes(x_ener.at[pl.ds(0, others)], e_sems.at[side])
         for c in range(FAST_CHUNKS):
             wait_bytes(x_send.at[pl.ds(0, others), :, spans[c]], g_sems.at[side, c])
@@ -398,6 +415,26 @@
         part = spans[c]
         pltpu.make_async_copy(x_send.at[others, :, part], g_out.at[my_tm, :, part], own_sems.at[1 + c]).wait()
     pltpu.make_async_copy(x_ener.at[others], e_out.at[my_tm], own_sems.at[1 + FAST_CHUNKS]).wait()
+
+
+def half_way(n_z, z_key):
+    half = n_z // 2
+    node = np.arange(n_z)
+    gap = (node[:, None] - node[None, :]) % n_z
+    count = jnp.sum((z_key[:, None, :] == node[None, :, None]).astype(jnp.int32), axis=2)
+    count = count.reshape(N_Y, 1, n_z * n_z)
+    busy = []
+    for way in range(2):
+        trip = gap if way == 0 else (-gap) % n_z
+        hops = gap.T if way == 0 else (-gap.T) % n_z
+        passes = (trip[None] < half) & (hops.T[:, None, :] < trip[None])
+        load = jnp.sum(jnp.where(passes.reshape(1, n_z, n_z * n_z), count, 0), axis=2)
+        near = (hops if way == 0 else hops) < half
+        busy.append(jnp.max(jnp.where(near[None], load[:, None, :], 0), axis=2))
+    opposite = (gap == half).reshape(n_z, n_z)
+    there = jnp.sum(jnp.where(opposite[None], count.reshape(N_Y, n_z, n_z), 0), axis=1)
+    even = ((np.arange(N_Y)[:, None] + node[None, :]) % 2 == 0).astype(np.int32)
+    return jnp.clip((there * 32 + 8 * (busy[1] - busy[0]) + 32 * even) // 64, 0, there)
 
 
 def routes(n_pair, blocks, my_pair, live, source, held, rank):
@@ -415,29 +452,32 @@
     y_tab = jnp.sum(jnp.where(place == want, held.reshape(N_Y, 1, n), 0), axis=2)
     y_tab = lax.dynamic_slice_in_dim(jnp.concatenate([y_tab, y_tab]), my_y + 1, N_Y - 1)
     ring_source = source.reshape(N_Y, n)
-    count = jnp.sum((ring_source[:, None, :] == rows[None, :, None]).astype(jnp.int32), axis=2)
-    leg = jnp.where(rows[None, :] // n_z == jnp.arange(N_Y)[:, None], 0, count)
+    ids = jnp.arange(n, dtype=jnp.int32)
+    earlier = ids[None, :] < ids[:, None]
+    y_same = (ring_source[:, :, None] == ring_source[:, None, :]) & earlier[None]
+    y_rank = jnp.sum(y_same.astype(jnp.int32), axis=2)
+    off_ring = live.reshape(N_Y, n) & (ring_source // n_z != jnp.arange(N_Y)[:, None])
+    y_over = jnp.where(off_ring, y_rank, 0) - (Y_CAP - 1)
 
     pos_in = jnp.arange(listed, dtype=jnp.int32)
     z_key = jnp.where(live, source % n_z, -1)
     z_same = (z_key[:, :, None] == z_key[:, None, :]) & (pos_in[None, :] < pos_in[:, None])[None]
     z_rank = jnp.sum(z_same.astype(jnp.int32), axis=2).reshape(N_Y, n)
-    ids = jnp.arange(n, dtype=jnp.int32)
     zd = ids // listed
     zs = ring_source % n_z
     delta = (zd[None, :] - zs) % n_z
     half = n_z // 2
-    plus = (delta < half) | ((delta == half) & ((z_rank + zs + jnp.arange(N_Y)[:, None]) % 2 == 0))
+    share = half_way(n_z, z_key)
+    mine_share = jnp.sum(jnp.where(zs[:, :, None] == jnp.arange(n_z)[None, None, :], share[:, None, :], 0), axis=2)
+    plus = (delta < half) | ((delta == half) & (z_rank < mine_share))
     way = jnp.where(plus, 0, 1)
     rem = jnp.where(live.reshape(N_Y, n), jnp.where(plus, delta, n_z - delta), 0)
     pos = zs
 
     ring = lambda v: lax.dynamic_index_in_dim(v, my_y, 0, keepdims=False)
     src, my_way = ring(ring_source), ring(way)
-    earlier = ids[None, :] < ids[:, None]
-    y_rank = jnp.sum(((src[:, None] == src[None, :]) & earlier).astype(jnp.int32), axis=1)
     step_y = (my_y - src // n_z) % N_Y
-    loc = jnp.where(step_y == 0, ring(held.reshape(N_Y, n)), blocks + (step_y - 1) * Y_CAP + y_rank)
+    loc = jnp.where(step_y == 0, ring(held.reshape(N_Y, n)), blocks + (step_y - 1) * Y_CAP + ring(y_rank))
     loc = jnp.where(src >= 0, loc, 0)
     total = sum(Z_CAPS)
     tables, begun = [], 0
@@ -457,30 +497,29 @@
         rem = rem - moved.astype(jnp.int32)
         begun += cap
     final = lax.dynamic_slice_in_dim(loc, my_z * listed, listed)
-    fits = jnp.maximum(jnp.max(rem), jnp.max(leg - Y_CAP)) <= 0
+    fits = jnp.maximum(jnp.max(rem), jnp.max(y_over)) <= 0
     return fits, y_tab.reshape(-1), jnp.concatenate(tables), final
 
 
-def entry_kernel(own, n_time, a_ref, g_ref, e_ref, tile_ref, cos_ref, tau_ref, live_ref, w_ref, c_ref, x_ref, y_ref):
+def entry_kernel(own, n_time, a_ref, g_ref, e_ref, tile_ref, cos_ref, tau_ref, live_ref, w_ref, c_ref, x_ref, y_ref, s_ref):
     e = pl.program_id(0)
     slices, _, size, width = a_ref.shape
     live = live_ref[e]
     lines = lambda v: jnp.concatenate([v[i : i + 1] for i in range(v.shape[0])], axis=1)
-    chi = [jnp.zeros((size, size), jnp.float32) for _ in range(n_time)]
     for m in range(slices):
-        eg = lines(e_ref[m, e])
-        ea = lines(e_ref[m, own + e])
-        a = a_ref[m, 0].astype(jnp.float32)
+        span = pl.ds(m * width, width)
+        x_ref[:, span] = a_ref[m, 0]
+        rate = lines(e_ref[m, e] + e_ref[m, own + e])
         g = g_ref[m, 0].astype(jnp.float32)
         for t in range(n_time):
-            x = (a * jnp.exp(-tau_ref[t] * ea)).astype(jnp.bfloat16)
-            y = (g * jnp.exp(-tau_ref[t] * eg)).astype(jnp.bfloat16)
-            x_ref[t, m] = x
-            y_ref[t, m] = y
-            chi[t] = chi[t] + lax.dot_general(
-                x, y, (((1,), (1,)), ((), ())), preferred_element_type=jnp.float32
-            )
-    chi = [c * live for c in chi]
+            decay = jnp.exp(-tau_ref[t] * rate)
+            s_ref[pl.ds(t, 1), span] = decay
+            y_ref[t, :, span] = (g * decay).astype(jnp.bfloat16)
+    chi = []
+    for t in range(n_time):
+        chi.append(live * lax.dot_general(
+            x_ref[...], y_ref[t], (((1,), (1,)), ((), ())), preferred_element_type=jnp.float32
+        ))
     wfreq = []
     for w in range(n_time):
         chiw = sum(cos_ref[w, t] * chi[t] for t in range(n_time)).astype(jnp.bfloat16)
@@ -489,16 +528,17 @@
         wfreq.append(
             prod + jnp.dot(prod_b, prod_b, preferred_element_type=jnp.float32) * (1.0 / math.sqrt(size))
         )
-    screened = []
     for t in range(n_time):
-        wt = (sum(cos_ref[w, t] * wfreq[w] for w in range(n_time)) * (1.0 / n_time)).astype(jnp.bfloat16)
-        w_ref[0, t] = wt
-        screened.append(wt)
+        w_ref[0, t] = (sum(cos_ref[w, t] * wfreq[w] for w in range(n_time)) * (1.0 / n_time)).astype(jnp.bfloat16)
+    screened = w_ref[0].reshape(n_time * size, size)
     for m in range(slices):
+        span = pl.ds(m * width, width)
+        wy = jnp.dot(screened, g_ref[m, 0], preferred_element_type=jnp.float32)
+        a = a_ref[m, 0].astype(jnp.float32)
         total = jnp.zeros((1, width), jnp.float32)
         for t in range(n_time):
-            wy = jnp.dot(screened[t], y_ref[t, m], preferred_element_type=jnp.float32)
-            total = total + jnp.sum(x_ref[t, m].astype(jnp.float32) * wy, axis=0, keepdims=True)
+            part = jnp.sum(a * wy[t * size : (t + 1) * size], axis=0, keepdims=True)
+            total = total + s_ref[pl.ds(t, 1), span] * part
         c_ref[0, pl.ds(m, 1), :] = total * (1.0 / n_time)
 
 
@@ -624,11 +664,12 @@
             out_shape=gathered,
             in_specs=[smem] + [vmem] * 2,
             out_specs=(hbm, hbm, hbm),
-            scratch_shapes=[pltpu.VMEM((N_Y - 1, Y_CAP, size, width), bf16)] * 2
-            + [pltpu.VMEM((2, total, size, width), bf16)] * 2
+            scratch_shapes=[pltpu.VMEM((N_Y - 1, Y_CAP * size, width), bf16)] * 2
+            + [pltpu.VMEM((2, total * size, width), bf16)] * 2
             + [
                 pltpu.VMEM((CAP * n_pair, width // LINE, LINE), jnp.float32),
                 pltpu.VMEM((CAP * n_pair, width // LINE, LINE), jnp.float32),
+                pltpu.VMEM((n_tm, own, size, width), bf16),
                 pltpu.VMEM((n_tm, own, size, width), bf16),
                 pltpu.VMEM((n_tm, 2 * own, width // LINE, LINE), jnp.float32),
             ]
@@ -697,7 +738,11 @@
             pl.BlockSpec((1, n_time, size, size), lambda e: (e, 0, 0, 0)),
             pl.BlockSpec((1, n_tm, width), lambda e: (e, 0, 0)),
         ),
-        scratch_shapes=[pltpu.VMEM((n_time, n_tm, size, width), bf16)] * 2,
+        scratch_shapes=[
+            pltpu.VMEM((size, n_tm * width), bf16),
+            pltpu.VMEM((n_time, size, n_tm * width), bf16),
+            pltpu.VMEM((8, n_tm * width), jnp.float32),
+        ],
         compiler_params=pltpu.CompilerParams(vmem_limit_bytes=48 * 1024 * 1024),
     )(a_all, g_all, e_all, coulomb[0], cosine, tau_grid, my_owned)
 

time: 213 us -> 204 us (0.958)
  Pallas kernels: 195 us -> 181 us
  other arithmetic: 9.42 us -> 13.6 us
    pallas_call x1, Pallas kernels: 167 us -> 152 us  [pooled(): pl.pallas_call(functools.partial(fast_kernel, n_tm, n_pair, own, size), o...]
    reduce_sum x3 -> x5, other arithmetic: 0.5 us -> 2.72 us  [the longest x1 0.91 us: half_way(): jnp.sum(jnp.where(passes.reshape(1, n_z, n_z * n_z), count, 0), axis=2)]
where the time goes in v4:
time: 204 us; the launch traced here: 203 us
  Pallas kernels  181 us (89%)
  other arithmetic  13.6 us (7%)
  local copies, waits for them, and re-layouts  5.7 us (3%)
  between operations  2.21 us (1%)
    pallas_call x1, Pallas kernels, pooled(): pl.pallas_call(functools.partial(fast_kernel, n_tm, n_pair, own, size), o...  152 us
    pallas_call x1, Pallas kernels, body(): pl.pallas_call(functools.partial(return_kernel, n_tm, n_pair, own), out_s...  14.9 us
    pallas_call x1, Pallas kernels, body(): pl.pallas_call(functools.partial(entry_kernel, own, n_time), grid=(own,),...  14.5 us

profile of v4, /device:TPU:1, one launch (start us, length us, event | category | flops | bytes accessed | tf_op | source)
XLA Modules:
  0.0 203.1 jit_solution(16212486692223496408)
XLA Ops:
  0.7 0.8 multiply_cosine_fusion.cos_ref
  1.5 0.1 ne.781
  1.6 0.9 fusion.86
  2.6 0.1 convert_reduce_fusion.9
  2.7 0.1 fusion.56.live_ref
  2.8 0.2 fusion.7
  3.0 1.4 convert_reduce_fusion.5
  4.4 0.1 convert_reduce_fusion.8
  4.7 0.1 select_reduce_fusion.3
  4.8 0.1 fusion.15
  4.9 0.5 fusion.52.back_ref
  6.0 0.3 select_reduce_fusion
  6.4 0.1 copy.21
  6.5 0.1 reshape.1227
  6.6 0.1 copy.22
  6.7 0.1 eq.553
  6.8 0.6 convert_reduce_fusion.7
  7.5 0.7 fusion.10
  8.2 0.9 select_reduce_fusion.14
  9.1 0.8 select_reduce_fusion.13
  10.0 0.8 select_reduce_fusion.15
  10.8 0.7 fusion.42
  11.5 0.1 select_reduce_fusion.2
  11.7 0.5 convert_reduce_fusion.4
  12.3 0.1 lt.436
  12.3 0.5 convert_reduce_fusion.3
  12.9 0.1 lt.439
  13.0 0.5 convert_reduce_fusion.2
  13.6 0.5 convert_reduce_fusion.1
  14.3 0.1 lt.446
  14.3 0.1 lt.443
  14.5 0.1 copy.20
  14.6 0.1 reshape.1226
  14.7 0.6 fusion.1.owning_ref
  15.3 0.8 reshape.1231
  16.1 0.4 convert_reduce_fusion
  16.7 0.1 select_reduce_fusion.4
  16.8 0.1 select_reduce_fusion.6
  17.0 0.1 select_reduce_fusion.8
  17.1 0.1 select_reduce_fusion.10
  17.2 0.1 concatenate.14
  17.4 0.7 add_reduce_fusion
  19.4 152.2 %conditional.1 = ((bf16[8,4,256,256]{3,2,1,0:T(8,128)(2,1)}, bf16[8,4,256,256]{3,2,1,0:T(8,128)(2,1)}, f32[8,8,2,128]{3,2,1,0:T(2,128)S(1)})) conditional(s32[]{:T(128)} %convert_element_type.156, (s32[285]{0:T(512)S(1)}, bf16[64,256,256]{2,1,0:T(8,128)(2,1)}, f32[64,2,128]{2,1,0:T(2,128)S(1)}) %tuple.14, (s32[285]{0:T(512)S(1)}, ...), branch_computations={%region_28.29_spmd, %region_29.30_spmd} | conditional | bytes 8 | solution.py:719
  19.4 152.0 %branch_1_fun.1 = (bf16[8,4,256,256]{3,2,1,0:T(8,128)(2,1)}, bf16[8,4,256,256]{3,2,1,0:T(8,128)(2,1)}, f32[8,8,2,128]{3,2,1,0:T(2,128)S(1)}) custom-call(s32[285]{0:T(512)S(1)} %get-tuple-element.15.table_ref, bf16[64,256,256]{2,1,0:T(8,128)(2,1)} %get-tuple-element.16.coef_ref, f32[64,2,128]{2,1,0:T(2,128)S(1)} %get-tuple-element.17.ener_ref), custom_call_target="tpu_custom_call" | custom-call | tf_op jit(solution)/shard_map/cond/branch_1_fun/pallas_call | solution.py:662
  171.6 14.5 %shard_map.140 = (bf16[4,3,256,256]{3,2,1,0:T(8,128)(2,1)}, f32[4,8,256]{2,1,0:T(8,128)S(1)}) custom-call(bf16[8,4,256,256]{3,2,1,0:T(8,128)(2,1)} %get-tuple-element.25.a_ref, bf16[8,4,256,256]{3,2,1,0:T(8,128)(2,1)} %get-tuple-element.26.g_ref, f32[8,8,2,128]{3,2,1,0:T(2,128)S(1)} %get-tuple-element.27.e_ref, bf16[4,256,256]{2,1,0:T(8,128)(2,1)S(1)} %bitcast.65, ...), custom_call_target="tpu_custom_call" | custom-call | tf_op jit(solution)/shard_map/pallas_call | solution.py:723
  186.1 0.6 copy-done.1
  186.7 14.9 %shard_map.141 = f32[64,256]{1,0:T(8,128)} custom-call(s32[64]{0:T(128)} %fusion.52.back_ref, f32[4,8,256]{2,1,0:T(8,128)} %copy-done.1, f32[64,64]{1,0:T(8,128)} %fusion.1.owning_ref), custom_call_target="tpu_custom_call" | custom-call | tf_op jit(solution)/shard_map/pallas_call | solution.py:749
  201.6 1.5 copy.31
  (49 shorter events, 1.7 us)
Async XLA Ops:
  19.4 152.2 %copy-start = (bf16[1,4,256,256]{3,2,1,0:T(8,128)(2,1)S(1)}, bf16[1,4,256,256]{3,2,1,0:T(8,128)(2,1)}, u32[]{:S(2)}) copy-start(bf16[1,4,256,256]{3,2,1,0:T(8,128)(2,1)} %param.17) | copy-start | bytes 1572868
  19.4 152.2 %copy-start.2 = (f32[3]{0:T(128)S(1)}, f32[3]{0:T(128)}, u32[]{:S(2)}) copy-start(f32[3]{0:T(128)} %tau_ref.1) | copy-start | bytes 40
  186.1 0.6 copy-start.1

commit v5 on v4

--- a/solution.py
+++ b/solution.py
@@ -200,9 +200,9 @@
 
 def fast_kernel(
     n_tm, n_pair, own, rows,
-    table_ref, coef_ref, ener_ref,
+    table_ref, coef_hbm, ener_ref,
     a_out, g_out, e_out,
-    y_send, y_recv, z_send, z_recv, e_send, e_recv, a_send, x_send, x_ener, *rest,
+    coef_ref, y_send, y_recv, z_send, z_recv, e_send, e_recv, a_send, x_send, x_ener, *rest,
 ):
     slot_ref, local_ref, pick_ref, final_ref, y_ref, z_ref = views(table_ref, n_tm * own, n_pair)
     pools = rest[:POOLS]
@@ -219,7 +219,10 @@
     y_slots = (N_Y - 1) * Y_CAP
     ahead = (my_y * n_z + lax.rem(my_z + 1, n_z), my_y * n_z + lax.rem(my_z + n_z - 1, n_z))
     firsts = [sum(Z_CAPS[:r]) for r in range(len(Z_CAPS) + 1)]
+    load = pltpu.make_async_copy(coef_hbm, coef_ref, own_sems.at[2 + FAST_CHUNKS])
+    load.start()
     greet(n_tm, n_pair, my_tm, my_pair)
+    load.wait()
 
     def ener_copy(i):
         target = lax.rem(my_pair + i + 1, n_pair)
@@ -421,18 +424,20 @@
     half = n_z // 2
     node = np.arange(n_z)
     gap = (node[:, None] - node[None, :]) % n_z
-    count = jnp.sum((z_key[:, None, :] == node[None, :, None]).astype(jnp.int32), axis=2)
-    count = count.reshape(N_Y, 1, n_z * n_z)
-    busy = []
+    count = jnp.sum((z_key[:, :, None] == node).astype(jnp.bfloat16), axis=1)
+    masks = []
     for way in range(2):
         trip = gap if way == 0 else (-gap) % n_z
-        hops = gap.T if way == 0 else (-gap.T) % n_z
-        passes = (trip[None] < half) & (hops.T[:, None, :] < trip[None])
-        load = jnp.sum(jnp.where(passes.reshape(1, n_z, n_z * n_z), count, 0), axis=2)
-        near = (hops if way == 0 else hops) < half
-        busy.append(jnp.max(jnp.where(near[None], load[:, None, :], 0), axis=2))
-    opposite = (gap == half).reshape(n_z, n_z)
-    there = jnp.sum(jnp.where(opposite[None], count.reshape(N_Y, n_z, n_z), 0), axis=1)
+        from_start = trip
+        passes = (trip[:, :, None] < half) & (from_start.T[None, :, :] < trip[:, :, None])
+        masks.append(passes.reshape(n_z * n_z, n_z))
+    opposite = (gap == half).reshape(n_z * n_z, 1) & (np.arange(n_z * n_z)[:, None] % n_z == node[None, :])
+    masks.append(opposite)
+    mask = jnp.asarray(np.concatenate(masks, axis=1), jnp.bfloat16)
+    sums = jnp.dot(count.reshape(N_Y, n_z * n_z), mask, preferred_element_type=jnp.float32).astype(jnp.int32)
+    up, down, there = sums[:, :n_z], sums[:, n_z : 2 * n_z], sums[:, 2 * n_z :]
+    most = lambda v, by: functools.reduce(jnp.maximum, [jnp.roll(v, by * h, axis=1) for h in range(half)])
+    busy = (most(up, -1), most(down, 1))
     even = ((np.arange(N_Y)[:, None] + node[None, :]) % 2 == 0).astype(np.int32)
     return jnp.clip((there * 32 + 8 * (busy[1] - busy[0]) + 32 * even) // 64, 0, there)
 
@@ -453,22 +458,22 @@
     y_tab = lax.dynamic_slice_in_dim(jnp.concatenate([y_tab, y_tab]), my_y + 1, N_Y - 1)
     ring_source = source.reshape(N_Y, n)
     ids = jnp.arange(n, dtype=jnp.int32)
-    earlier = ids[None, :] < ids[:, None]
+    earlier = ids[:, None] < ids[None, :]
     y_same = (ring_source[:, :, None] == ring_source[:, None, :]) & earlier[None]
-    y_rank = jnp.sum(y_same.astype(jnp.int32), axis=2)
+    y_rank = jnp.sum(y_same.astype(jnp.int32), axis=1)
     off_ring = live.reshape(N_Y, n) & (ring_source // n_z != jnp.arange(N_Y)[:, None])
     y_over = jnp.where(off_ring, y_rank, 0) - (Y_CAP - 1)
 
     pos_in = jnp.arange(listed, dtype=jnp.int32)
     z_key = jnp.where(live, source % n_z, -1)
-    z_same = (z_key[:, :, None] == z_key[:, None, :]) & (pos_in[None, :] < pos_in[:, None])[None]
-    z_rank = jnp.sum(z_same.astype(jnp.int32), axis=2).reshape(N_Y, n)
+    z_same = (z_key[:, :, None] == z_key[:, None, :]) & (pos_in[:, None] < pos_in[None, :])[None]
+    z_rank = jnp.sum(z_same.astype(jnp.int32), axis=1).reshape(N_Y, n)
     zd = ids // listed
     zs = ring_source % n_z
     delta = (zd[None, :] - zs) % n_z
     half = n_z // 2
     share = half_way(n_z, z_key)
-    mine_share = jnp.sum(jnp.where(zs[:, :, None] == jnp.arange(n_z)[None, None, :], share[:, None, :], 0), axis=2)
+    mine_share = jnp.sum(jnp.where(zs[None] == jnp.arange(n_z)[:, None, None], share.T[:, :, None], 0), axis=0)
     plus = (delta < half) | ((delta == half) & (z_rank < mine_share))
     way = jnp.where(plus, 0, 1)
     rem = jnp.where(live.reshape(N_Y, n), jnp.where(plus, delta, n_z - delta), 0)
@@ -485,8 +490,8 @@
     for cap in Z_CAPS:
         group = jnp.where(rem > 0, pos * 2 + way, -1)
         key = rem * n - ids[None, :]
-        ahead = (group[:, :, None] == group[:, None, :]) & (key[:, None, :] > key[:, :, None])
-        order = jnp.sum(ahead.astype(jnp.int32), axis=2)
+        ahead = (group[:, :, None] == group[:, None, :]) & (key[:, :, None] > key[:, None, :])
+        order = jnp.sum(ahead.astype(jnp.int32), axis=1)
         moved = (rem > 0) & (order < cap)
         my_order, my_moved, my_group = ring(order), ring(moved), ring(group)
         for w in range(2):
@@ -617,8 +622,8 @@
     source = jnp.where(live, remote // blocks, -1)
     held = remote % blocks
     pos = jnp.arange(listed, dtype=jnp.int32)
-    before = (source[:, :, None] == source[:, None, :]) & (pos[None, :] < pos[:, None])[None]
-    rank = jnp.sum(before.astype(jnp.int32), axis=2)
+    before = (source[:, :, None] == source[:, None, :]) & (pos[:, None] < pos[None, :])[None]
+    rank = jnp.sum(before.astype(jnp.int32), axis=1)
     slots = jnp.arange(CAP, dtype=jnp.int32)
     hit = (source == my_pair)[:, None, :] & (rank[:, None, :] == slots[None, :, None])
     pick = jnp.sum(jnp.where(hit, held[:, None, :], 0), axis=2)
@@ -662,9 +667,10 @@
         return pl.pallas_call(
             functools.partial(fast_kernel, n_tm, n_pair, own, size),
             out_shape=gathered,
-            in_specs=[smem] + [vmem] * 2,
+            in_specs=[smem, hbm, vmem],
             out_specs=(hbm, hbm, hbm),
-            scratch_shapes=[pltpu.VMEM((N_Y - 1, Y_CAP * size, width), bf16)] * 2
+            scratch_shapes=[pltpu.VMEM((blocks, size, width), bf16)]
+            + [pltpu.VMEM((N_Y - 1, Y_CAP * size, width), bf16)] * 2
             + [pltpu.VMEM((2, total * size, width), bf16)] * 2
             + [
                 pltpu.VMEM((CAP * n_pair, width // LINE, LINE), jnp.float32),
@@ -684,7 +690,7 @@
                 DMA((2,)),
                 DMA((2, FAST_CHUNKS)),
                 DMA((2,)),
-                DMA((2 + FAST_CHUNKS,)),
+                DMA((3 + FAST_CHUNKS,)),
             ],
             compiler_params=pltpu.CompilerParams(
                 collective_id=2, has_side_effects=True, vmem_limit_bytes=62 * 1024 * 1024

time: 204 us -> 196 us (0.961)
  other arithmetic: 13.6 us -> 8.05 us
  Pallas kernels: 181 us -> 178 us
    reduce_sum x10 -> x8, other arithmetic: 6.26 us -> 2.26 us  [the longest x4 1.41 us: routes(): order = jnp.sum(ahead.astype(jnp.int32), axis=1)]
    pallas_call x1, Pallas kernels: 152 us -> 148 us  [pooled(): pl.pallas_call(functools.partial(fast_kernel, n_tm, n_pair, own, size), o...]
where the time goes in v5:
time: 196 us
  Pallas kernels  178 us (91%)
  other arithmetic  8.05 us (4%)
  local copies, waits for them, and re-layouts  6.14 us (3%)
  between operations  2.22 us (1%)
    pallas_call x1, Pallas kernels, pooled(): pl.pallas_call(functools.partial(fast_kernel, n_tm, n_pair, own, size), o...  148 us
    pallas_call x1, Pallas kernels, body(): pl.pallas_call(functools.partial(return_kernel, n_tm, n_pair, own), out_s...  15.3 us
    pallas_call x1, Pallas kernels, body(): pl.pallas_call(functools.partial(entry_kernel, own, n_time), grid=(own,),...  14.5 us

profile of v5, /device:TPU:1, one launch (start us, length us, event | category | flops | bytes accessed | tf_op | source)
XLA Modules:
  0.0 195.7 jit_solution(17999496682474544883)
XLA Ops:
  0.7 0.8 multiply_cosine_fusion.cos_ref
  1.5 0.1 ne.785
  1.6 0.9 fusion.97
  2.6 0.1 fusion.1
  2.7 0.1 reshape.1258
  2.8 0.8 convolution_convert_fusion
  4.1 0.8 fusion.45
  4.8 0.1 convert_reduce_fusion.8
  5.0 0.1 fusion.67.live_ref
  5.1 0.2 fusion.9
  5.3 0.4 convert_reduce_fusion.5
  5.7 0.1 convert_reduce_fusion.7
  6.0 0.1 select_reduce_fusion.3
  6.0 0.1 fusion.17
  6.1 0.5 fusion.63.back_ref
  6.8 0.1 add.700
  7.3 0.3 select_reduce_fusion
  7.6 0.1 dynamic-slice_add_fusion
  7.7 0.1 copy.20
  7.8 0.1 reshape.1261
  7.9 0.1 select_reduce_fusion.2
  8.0 0.4 convert_reduce_fusion.4
  8.5 0.1 lt.436
  8.6 0.4 convert_reduce_fusion.3
  9.0 0.1 lt.439
  9.1 0.4 convert_reduce_fusion.2
  9.5 0.4 convert_reduce_fusion.1
  10.0 0.1 lt.446
  10.0 0.1 lt.443
  10.2 0.1 copy.21
  10.3 0.1 eq.550
  10.4 0.1 copy.19
  10.5 0.1 reshape.1260
  10.6 0.6 fusion.3.owning_ref
  11.2 0.8 reshape.1265
  12.0 0.2 convert_reduce_fusion
  12.5 0.1 select_reduce_fusion.4
  12.6 0.1 select_reduce_fusion.6
  12.7 0.1 select_reduce_fusion.8
  12.8 0.1 select_reduce_fusion.10
  12.9 0.1 concatenate.44
  13.1 0.7 add_reduce_fusion
  15.1 148.7 %conditional.1 = ((bf16[8,4,256,256]{3,2,1,0:T(8,128)(2,1)}, bf16[8,4,256,256]{3,2,1,0:T(8,128)(2,1)}, f32[8,8,2,128]{3,2,1,0:T(2,128)S(1)})) conditional(s32[]{:T(128)} %convert_element_type.162, (s32[285]{0:T(512)S(1)}, bf16[64,256,256]{2,1,0:T(8,128)(2,1)}, f32[64,2,128]{2,1,0:T(2,128)S(1)}) %tuple.14, (s32[285]{0:T(512)S(1)}, ...), branch_computations={%region_23.24_spmd, %region_24.25_spmd} | conditional | bytes 8 | solution.py:725
  15.2 148.5 %branch_1_fun.1 = (bf16[8,4,256,256]{3,2,1,0:T(8,128)(2,1)}, bf16[8,4,256,256]{3,2,1,0:T(8,128)(2,1)}, f32[8,8,2,128]{3,2,1,0:T(2,128)S(1)}) custom-call(s32[285]{0:T(512)S(1)} %get-tuple-element.15.table_ref, bf16[64,256,256]{2,1,0:T(8,128)(2,1)} %get-tuple-element.16.coef_hbm, f32[64,2,128]{2,1,0:T(2,128)S(1)} %get-tuple-element.17.ener_ref), custom_call_target="tpu_custom_call" | custom-call | tf_op jit(solution)/shard_map/cond/branch_1_fun/pallas_call | solution.py:667
  163.8 14.5 %shard_map.104 = (bf16[4,3,256,256]{3,2,1,0:T(8,128)(2,1)}, f32[4,8,256]{2,1,0:T(8,128)S(1)}) custom-call(bf16[8,4,256,256]{3,2,1,0:T(8,128)(2,1)} %get-tuple-element.25.a_ref, bf16[8,4,256,256]{3,2,1,0:T(8,128)(2,1)} %get-tuple-element.26.g_ref, f32[8,8,2,128]{3,2,1,0:T(2,128)S(1)} %get-tuple-element.27.e_ref, bf16[4,256,256]{2,1,0:T(8,128)(2,1)S(1)} %bitcast.65, ...), custom_call_target="tpu_custom_call" | custom-call | tf_op jit(solution)/shard_map/pallas_call | solution.py:729
  178.3 0.6 copy-done.1
  178.9 15.3 %shard_map.105 = f32[64,256]{1,0:T(8,128)} custom-call(s32[64]{0:T(128)} %fusion.63.back_ref, f32[4,8,256]{2,1,0:T(8,128)} %copy-done.1, f32[64,64]{1,0:T(8,128)} %fusion.3.owning_ref), custom_call_target="tpu_custom_call" | custom-call | tf_op jit(solution)/shard_map/pallas_call | solution.py:755
  194.3 1.5 copy.30
  (52 shorter events, 1.9 us)
Async XLA Ops:
  15.1 148.7 %copy-start = (bf16[1,4,256,256]{3,2,1,0:T(8,128)(2,1)S(1)}, bf16[1,4,256,256]{3,2,1,0:T(8,128)(2,1)}, u32[]{:S(2)}) copy-start(bf16[1,4,256,256]{3,2,1,0:T(8,128)(2,1)} %param.13) | copy-start | bytes 1572868
  15.1 148.7 %copy-start.2 = (f32[3]{0:T(128)S(1)}, f32[3]{0:T(128)}, u32[]{:S(2)}) copy-start(f32[3]{0:T(128)} %tau_ref.1) | copy-start | bytes 40
  178.3 0.6 copy-start.1

commit v6 on v5

--- a/solution.py
+++ b/solution.py
@@ -36,7 +36,7 @@
 
     lax.fori_loop(1, n_pair, pair_peer, 0)
     lax.fori_loop(1, n_tm, tm_peer, 0)
-    pl.semaphore_wait(barrier, n_pair + n_tm - 2)
+    return lambda: pl.semaphore_wait(barrier, n_pair + n_tm - 2)
 
 
 class View:
@@ -53,13 +53,19 @@
     return [View(table, i) for i in at]
 
 
+def spread(flat_ref, tile_ref):
+    flat = flat_ref[...].astype(jnp.float32)
+    for h in range(flat.shape[1] // LINE):
+        tile_ref[:, h, :] = flat[:, h * LINE : (h + 1) * LINE]
+
+
 def wait_bytes(ref, sem):
     pltpu.make_async_copy(ref, ref, sem).wait()
 
 
 def gather_kernel(
     n_tm, n_pair, own, rows,
-    table_ref, coef_ref, ener_ref,
+    table_ref, coef_ref, ener_in,
     a_out, g_out, e_out,
     *scratch,
 ):
@@ -67,10 +73,11 @@
     my_tm, my_pair = lax.axis_index("tm"), lax.axis_index("pair")
     sends, recvs = scratch[:CHUNKS], scratch[CHUNKS : 2 * CHUNKS]
     (e_send, e_recv, a_send, g_send, x_ener,
-     pair_send, pair_recv, a_sems, g_sems, e_sems, own_sems) = scratch[2 * CHUNKS :]
+     pair_send, pair_recv, a_sems, g_sems, e_sems, own_sems, ener_ref) = scratch[2 * CHUNKS :]
     peers, others = n_pair - 1, n_tm - 1
     step = rows // CHUNKS
-    greet(n_tm, n_pair, my_tm, my_pair)
+    spread(ener_in, ener_ref)
+    greet(n_tm, n_pair, my_tm, my_pair)()
 
     def pair_copy(i, c):
         target = lax.rem(my_pair + i + 1, n_pair)
@@ -200,9 +207,9 @@
 
 def fast_kernel(
     n_tm, n_pair, own, rows,
-    table_ref, coef_hbm, ener_ref,
+    table_ref, coef_hbm, ener_in,
     a_out, g_out, e_out,
-    coef_ref, y_send, y_recv, z_send, z_recv, e_send, e_recv, a_send, x_send, x_ener, *rest,
+    coef_ref, ener_ref, y_send, y_recv, z_send, z_recv, e_send, e_recv, a_send, x_send, x_ener, *rest,
 ):
     slot_ref, local_ref, pick_ref, final_ref, y_ref, z_ref = views(table_ref, n_tm * own, n_pair)
     pools = rest[:POOLS]
@@ -221,7 +228,8 @@
     firsts = [sum(Z_CAPS[:r]) for r in range(len(Z_CAPS) + 1)]
     load = pltpu.make_async_copy(coef_hbm, coef_ref, own_sems.at[2 + FAST_CHUNKS])
     load.start()
-    greet(n_tm, n_pair, my_tm, my_pair)
+    met = greet(n_tm, n_pair, my_tm, my_pair)
+    spread(ener_in, ener_ref)
     load.wait()
 
     def ener_copy(i):
@@ -242,19 +250,26 @@
         for j in range(CAP * peers, CAP * n_pair):
             e_recv[j] = ener_ref[pick_ref[j]]
 
-    def send_y(c):
+    def stage_y(c):
         for i in range(N_Y - 1):
             def one(j, carry):
                 y_send[i, pl.ds(pl.multiple_of(Y_CAP * begin[c] + j * PARTS[c], 16), PARTS[c]), :] = coef_ref[y_ref[i * Y_CAP + j], spans[c], :]
                 return carry
 
             lax.fori_loop(0, Y_CAP, one, 0)
+
+    def start_y(c):
+        for i in range(N_Y - 1):
             target = lax.rem(my_y + i + 1, N_Y) * n_z + my_z
             pltpu.make_async_remote_copy(
                 src_ref=y_send.at[i, y_rows[c]], dst_ref=y_recv.at[i, y_rows[c]],
                 send_sem=y_ssem, recv_sem=y_rsem.at[c],
                 device_id=(my_tm, target), device_id_type=MESH,
             ).start()
+
+    def send_y(c):
+        stage_y(c)
+        start_y(c)
 
     def fill(c):
         pool = pools[c % POOLS]
@@ -369,7 +384,9 @@
 
     last = len(Z_CAPS) - 1
     sent_ener = False
-    send_y(0)
+    stage_y(0)
+    met()
+    start_y(0)
     send_y(1)
     fill(0)
     send_z(0, 0)
@@ -549,15 +566,15 @@
 
 def return_kernel(
     n_tm, n_pair, own,
-    back_ref, contrib_ref, owning_ref,
+    back_ref, contrib_ref, given_ref,
     out_ref,
     c_send, c_recv, p_send, p_recv, tm_sems, pair_sems,
 ):
     my_tm, my_pair = lax.axis_index("tm"), lax.axis_index("pair")
     peers, others = n_pair - 1, n_tm - 1
     width = out_ref.shape[1]
+    met = greet(n_tm, n_pair, my_tm, my_pair)
     c_send[...] = jnp.zeros_like(c_send)
-    greet(n_tm, n_pair, my_tm, my_pair)
 
     def stage_c(u):
         owner = lax.rem(my_tm + u + 1, n_tm)
@@ -566,7 +583,7 @@
         return owner
 
     def tm_one(u, carry):
-        owner = stage_c(u)
+        owner = lax.rem(my_tm + u + 1, n_tm)
         pltpu.make_async_remote_copy(
             src_ref=c_send.at[u], dst_ref=c_recv.at[u],
             send_sem=tm_sems.at[0], recv_sem=tm_sems.at[1],
@@ -574,8 +591,12 @@
         ).start()
         return carry
 
+    for u in range(n_tm):
+        stage_c(u)
+    met()
     lax.fori_loop(0, others, tm_one, 0)
-    stage_c(others)
+    block_id = lax.broadcasted_iota(jnp.int32, (out_ref.shape[0], CAP * n_pair), 0)
+    owning = (block_id == given_ref[...]).astype(jnp.float32)
     wait_bytes(c_recv.at[pl.ds(0, others)], tm_sems.at[1])
     c_recv[others] = c_send[others]
 
@@ -605,7 +626,7 @@
         p_recv[j] = p_send[j]
     for h in range(width // LINE):
         out_ref[:, pl.ds(h * LINE, LINE)] = jnp.dot(
-            owning_ref[...], p_recv[:, h, :], precision=lax.Precision.HIGHEST, preferred_element_type=jnp.float32
+            owning, p_recv[:, h, :], precision=lax.Precision.HIGHEST, preferred_element_type=jnp.float32
         )
     wait_bytes(c_send.at[pl.ds(0, others)], tm_sems.at[0])
     wait_bytes(p_send.at[pl.ds(0, CAP * peers)], pair_sems.at[0])
@@ -641,10 +662,8 @@
     back = ((my_tm - back // own + n_tm - 1) % n_tm) * own + back % own
     back = jnp.where(jnp.any(match, axis=1), back, -1)
     given = jnp.where(used > 0, pick, -1).reshape(1, -1)
-    owning = (jnp.arange(blocks, dtype=jnp.int32)[:, None] == given).astype(jnp.float32)
     my_owned = lax.dynamic_slice_in_dim(my_live, my_tm * own, own).astype(jnp.float32)
     cosine = jnp.cos(freq_grid[:, None] * tau_grid[None, :])
-    lined = energies.astype(jnp.float32).reshape(blocks, width // LINE, LINE)
 
     smem = pl.BlockSpec(memory_space=pltpu.SMEM)
     vmem = pl.BlockSpec(memory_space=pltpu.VMEM)
@@ -661,7 +680,7 @@
     fits, y_tab, z_tab, final = routes(n_pair, blocks, my_pair, live, source, held, rank)
     table = jnp.concatenate([slot, my_local, pick.reshape(-1), final, y_tab, z_tab]).astype(jnp.int32)
 
-    def pooled(table, coefs, lined):
+    def pooled(table, coefs, energies):
         total = sum(Z_CAPS)
         depth = blocks + (N_Y - 1) * Y_CAP + 2 * total
         return pl.pallas_call(
@@ -669,7 +688,10 @@
             out_shape=gathered,
             in_specs=[smem, hbm, vmem],
             out_specs=(hbm, hbm, hbm),
-            scratch_shapes=[pltpu.VMEM((blocks, size, width), bf16)]
+            scratch_shapes=[
+                pltpu.VMEM((blocks, size, width), bf16),
+                pltpu.VMEM((blocks, width // LINE, LINE), jnp.float32),
+            ]
             + [pltpu.VMEM((N_Y - 1, Y_CAP * size, width), bf16)] * 2
             + [pltpu.VMEM((2, total * size, width), bf16)] * 2
             + [
@@ -695,9 +717,9 @@
             compiler_params=pltpu.CompilerParams(
                 collective_id=2, has_side_effects=True, vmem_limit_bytes=62 * 1024 * 1024
             ),
-        )(table, coefs, lined)
-
-    def direct(table, coefs, lined):
+        )(table, coefs, energies)
+
+    def direct(table, coefs, energies):
         return pl.pallas_call(
             functools.partial(gather_kernel, n_tm, n_pair, own, size),
             out_shape=gathered,
@@ -716,14 +738,15 @@
                 DMA((2, CHUNKS)),
                 DMA((2,)),
                 DMA((2 + CHUNKS,)),
+                pltpu.VMEM((blocks, width // LINE, LINE), jnp.float32),
             ],
             compiler_params=pltpu.CompilerParams(
                 collective_id=0, has_side_effects=True, vmem_limit_bytes=56 * 1024 * 1024
             ),
-        )(table, coefs, lined)
+        )(table, coefs, energies)
 
     a_all, g_all, e_all = lax.cond(
-        fits, pooled, direct, table, coefs, lined
+        fits, pooled, direct, table, coefs, energies
     )
 
     screened, contrib = pl.pallas_call(
@@ -766,7 +789,7 @@
             DMA((2,)),
         ],
         compiler_params=pltpu.CompilerParams(collective_id=1, has_side_effects=True),
-    )(back, contrib, owning)
+    )(back, contrib, given)
     return (screened[None], self_energy)
 
 

time: 196 us -> 195 us (level)
  no operation moved by 1% of the time
where the time goes in v6:
time: 195 us
  Pallas kernels  178 us (91%)
  other arithmetic  7.4 us (4%)
  local copies, waits for them, and re-layouts  5.88 us (3%)
  between operations  2.21 us (1%)
    pallas_call x1, Pallas kernels, pooled(): pl.pallas_call(functools.partial(fast_kernel, n_tm, n_pair, own, size), o...  148 us
    pallas_call x1, Pallas kernels, body(): pl.pallas_call(functools.partial(return_kernel, n_tm, n_pair, own), out_s...  16.3 us
    pallas_call x1, Pallas kernels, body(): pl.pallas_call(functools.partial(entry_kernel, own, n_time), grid=(own,),...  14.5 us

profile of v6, /device:TPU:1, one launch (start us, length us, event | category | flops | bytes accessed | tf_op | source)
XLA Modules:
  0.0 194.9 jit_solution(4264162279947777451)
XLA Ops:
  0.7 0.8 multiply_cosine_fusion.cos_ref
  1.5 0.1 ne.785
  1.6 0.9 fusion.96
  2.6 0.1 fusion.1
  2.7 0.1 reshape.1253
  2.8 0.8 convolution_convert_fusion
  4.1 0.8 fusion.44
  4.8 0.1 convert_reduce_fusion.8
  5.0 0.1 fusion.66.live_ref
  5.1 0.2 fusion.8
  5.3 0.4 convert_reduce_fusion.5
  5.7 0.1 convert_reduce_fusion.7
  6.0 0.1 select_reduce_fusion.3
  6.1 0.1 fusion.16
  6.1 0.5 fusion.62.back_ref
  6.8 0.1 add.700
  7.1 0.1 add.702
  7.2 0.3 select_reduce_fusion
  7.6 0.1 dynamic-slice_add_fusion
  7.7 0.1 copy.20
  7.7 0.1 reshape.1256
  7.8 0.1 select_reduce_fusion.2
  8.0 0.4 convert_reduce_fusion.4
  8.4 0.1 lt.436
  8.5 0.4 convert_reduce_fusion.3
  8.9 0.1 lt.439
  9.0 0.4 convert_reduce_fusion.2
  9.5 0.4 convert_reduce_fusion.1
  9.9 0.1 lt.446
  10.0 0.1 lt.443
  10.2 0.1 copy.21
  10.3 0.6 reshape.1257.given_ref
  10.9 0.1 copy.19
  11.0 0.1 reshape.1255
  11.1 0.2 convert_reduce_fusion
  11.5 0.1 dynamic_slice.97
  11.5 0.1 select_reduce_fusion.4
  11.7 0.1 select_reduce_fusion.6
  11.8 0.1 select_reduce_fusion.8
  11.9 0.1 select_reduce_fusion.10
  12.0 0.1 concatenate.44
  12.2 0.7 add_reduce_fusion
  14.2 147.8 %conditional.1 = ((bf16[8,4,256,256]{3,2,1,0:T(8,128)(2,1)}, bf16[8,4,256,256]{3,2,1,0:T(8,128)(2,1)}, f32[8,8,2,128]{3,2,1,0:T(2,128)S(1)})) conditional(s32[]{:T(128)} %convert_element_type.158, (s32[285]{0:T(512)S(1)}, bf16[64,256,256]{2,1,0:T(8,128)(2,1)}, bf16[64,256]{1,0:T(8,128)(2,1)}) %tuple.14, (s32[285]{0:T(512)S(1)}, ...), branch_computations={%region_23.24_spmd, %region_24.25_spmd} | conditional | bytes 8 | solution.py:748
  14.2 147.6 %branch_1_fun.1 = (bf16[8,4,256,256]{3,2,1,0:T(8,128)(2,1)}, bf16[8,4,256,256]{3,2,1,0:T(8,128)(2,1)}, f32[8,8,2,128]{3,2,1,0:T(2,128)S(1)}) custom-call(s32[285]{0:T(512)S(1)} %get-tuple-element.15.table_ref, bf16[64,256,256]{2,1,0:T(8,128)(2,1)} %get-tuple-element.16.coef_hbm, bf16[64,256]{1,0:T(8,128)(2,1)} %get-tuple-element.17.ener_in), custom_call_target="tpu_custom_call" | custom-call | tf_op jit(solution)/shard_map/cond/branch_1_fun/pallas_call | solution.py:686
  162.1 14.5 %shard_map.104 = (bf16[4,3,256,256]{3,2,1,0:T(8,128)(2,1)}, f32[4,8,256]{2,1,0:T(8,128)S(1)}) custom-call(bf16[8,4,256,256]{3,2,1,0:T(8,128)(2,1)} %get-tuple-element.25.a_ref, bf16[8,4,256,256]{3,2,1,0:T(8,128)(2,1)} %get-tuple-element.26.g_ref, f32[8,8,2,128]{3,2,1,0:T(2,128)S(1)} %get-tuple-element.27.e_ref, bf16[4,256,256]{2,1,0:T(8,128)(2,1)S(1)} %bitcast.65, ...), custom_call_target="tpu_custom_call" | custom-call | tf_op jit(solution)/shard_map/pallas_call | solution.py:752
  176.6 0.6 copy-done.1
  177.2 16.3 %shard_map.105 = f32[64,256]{1,0:T(8,128)} custom-call(s32[64]{0:T(128)} %fusion.62.back_ref, f32[4,8,256]{2,1,0:T(8,128)} %copy-done.1, s32[1,64]{1,0:T(1,128)} %reshape.1257.given_ref), custom_call_target="tpu_custom_call" | custom-call | tf_op jit(solution)/shard_map/pallas_call | solution.py:778
  193.5 1.5 copy.30
  (50 shorter events, 1.7 us)
Async XLA Ops:
  14.2 147.9 %copy-start = (bf16[1,4,256,256]{3,2,1,0:T(8,128)(2,1)S(1)}, bf16[1,4,256,256]{3,2,1,0:T(8,128)(2,1)}, u32[]{:S(2)}) copy-start(bf16[1,4,256,256]{3,2,1,0:T(8,128)(2,1)} %param.13) | copy-start | bytes 1572868
  14.2 147.9 %copy-start.2 = (f32[3]{0:T(128)S(1)}, f32[3]{0:T(128)}, u32[]{:S(2)}) copy-start(f32[3]{0:T(128)} %tau_ref.1) | copy-start | bytes 40
  176.6 0.6 copy-start.1

commit v7 on v6

--- a/solution.py
+++ b/solution.py
@@ -11,10 +11,10 @@
 
 CAP = 2
 CHUNKS = 4
-PARTS = (16, 16, 32, 32, 32, 32, 32, 32, 16, 16)
+PARTS = (32,) * 8
 FAST_CHUNKS = len(PARTS)
 Y_CAP = 15
-Z_CAPS = (10, 10, 9, 8)
+Z_CAPS = (10, 9, 9, 8)
 LINE = 128
 N_Y = 4
 POOLS = 3

time: 195 us -> 193 us (0.990)
  Pallas kernels: 178 us -> 176 us
where the time goes in v7:
time: 193 us; the launch traced here: 192 us
  Pallas kernels  176 us (91%)
  other arithmetic  7.4 us (4%)
  local copies, waits for them, and re-layouts  5.88 us (3%)
  between operations  2.21 us (1%)
    pallas_call x1, Pallas kernels, pooled(): pl.pallas_call(functools.partial(fast_kernel, n_tm, n_pair, own, size), o...  146 us
    pallas_call x1, Pallas kernels, body(): pl.pallas_call(functools.partial(return_kernel, n_tm, n_pair, own), out_s...  15.4 us
    pallas_call x1, Pallas kernels, body(): pl.pallas_call(functools.partial(entry_kernel, own, n_time), grid=(own,),...  14.5 us

profile of v7, /device:TPU:1, one launch (start us, length us, event | category | flops | bytes accessed | tf_op | source)
XLA Modules:
  0.0 192.4 jit_solution(545489079041987431)
XLA Ops:
  0.7 0.8 multiply_cosine_fusion.cos_ref
  1.5 0.1 ne.785
  1.6 0.9 fusion.96
  2.5 0.1 squeeze.55
  2.6 0.1 fusion.1
  2.7 0.1 reshape.1253
  2.8 0.8 convolution_convert_fusion
  4.1 0.8 fusion.44
  4.8 0.1 convert_reduce_fusion.8
  5.0 0.1 fusion.66.live_ref
  5.1 0.2 fusion.8
  5.3 0.4 convert_reduce_fusion.5
  5.7 0.1 convert_reduce_fusion.7
  6.0 0.1 select_reduce_fusion.3
  6.1 0.1 fusion.16
  6.1 0.5 fusion.62.back_ref
  6.8 0.1 add.700
  7.1 0.1 add.702
  7.2 0.3 select_reduce_fusion
  7.6 0.1 dynamic-slice_add_fusion
  7.7 0.1 copy.20
  7.7 0.1 reshape.1256
  7.8 0.1 select_reduce_fusion.2
  8.0 0.4 convert_reduce_fusion.4
  8.4 0.1 lt.437
  8.5 0.4 convert_reduce_fusion.3
  8.9 0.1 lt.440
  9.0 0.4 convert_reduce_fusion.2
  9.5 0.4 convert_reduce_fusion.1
  9.9 0.1 lt.446
  10.0 0.1 lt.443
  10.2 0.1 copy.21
  10.3 0.6 reshape.1257.given_ref
  10.9 0.1 copy.19
  11.0 0.1 reshape.1255
  11.1 0.2 convert_reduce_fusion
  11.5 0.1 select_reduce_fusion.4
  11.7 0.1 select_reduce_fusion.6
  11.8 0.1 select_reduce_fusion.8
  11.9 0.1 select_reduce_fusion.10
  12.0 0.1 concatenate.44
  12.2 0.7 add_reduce_fusion
  14.2 146.1 %conditional.1 = ((bf16[8,4,256,256]{3,2,1,0:T(8,128)(2,1)}, bf16[8,4,256,256]{3,2,1,0:T(8,128)(2,1)}, f32[8,8,2,128]{3,2,1,0:T(2,128)S(1)})) conditional(s32[]{:T(128)} %convert_element_type.158, (s32[285]{0:T(512)S(1)}, bf16[64,256,256]{2,1,0:T(8,128)(2,1)}, bf16[64,256]{1,0:T(8,128)(2,1)}) %tuple.14, (s32[285]{0:T(512)S(1)}, ...), branch_computations={%region_23.24_spmd, %region_24.25_spmd} | conditional | bytes 8 | solution.py:748
  14.2 146.1 %branch_1_fun.1 = (bf16[8,4,256,256]{3,2,1,0:T(8,128)(2,1)}, bf16[8,4,256,256]{3,2,1,0:T(8,128)(2,1)}, f32[8,8,2,128]{3,2,1,0:T(2,128)S(1)}) custom-call(s32[285]{0:T(512)S(1)} %get-tuple-element.15.table_ref, bf16[64,256,256]{2,1,0:T(8,128)(2,1)} %get-tuple-element.16.coef_hbm, bf16[64,256]{1,0:T(8,128)(2,1)} %get-tuple-element.17.ener_in), custom_call_target="tpu_custom_call" | custom-call | tf_op jit(solution)/shard_map/cond/branch_1_fun/pallas_call | solution.py:686
  160.4 14.5 %shard_map.104 = (bf16[4,3,256,256]{3,2,1,0:T(8,128)(2,1)}, f32[4,8,256]{2,1,0:T(8,128)S(1)}) custom-call(bf16[8,4,256,256]{3,2,1,0:T(8,128)(2,1)} %get-tuple-element.25.a_ref, bf16[8,4,256,256]{3,2,1,0:T(8,128)(2,1)} %get-tuple-element.26.g_ref, f32[8,8,2,128]{3,2,1,0:T(2,128)S(1)} %get-tuple-element.27.e_ref, bf16[4,256,256]{2,1,0:T(8,128)(2,1)S(1)} %bitcast.65, ...), custom_call_target="tpu_custom_call" | custom-call | tf_op jit(solution)/shard_map/pallas_call | solution.py:752
  174.9 0.6 copy-done.1
  175.5 15.4 %shard_map.105 = f32[64,256]{1,0:T(8,128)} custom-call(s32[64]{0:T(128)} %fusion.62.back_ref, f32[4,8,256]{2,1,0:T(8,128)} %copy-done.1, s32[1,64]{1,0:T(1,128)} %reshape.1257.given_ref), custom_call_target="tpu_custom_call" | custom-call | tf_op jit(solution)/shard_map/pallas_call | solution.py:778
  190.9 1.5 copy.30
  (50 shorter events, 1.7 us)
Async XLA Ops:
  14.2 146.2 %copy-start = (bf16[1,4,256,256]{3,2,1,0:T(8,128)(2,1)S(1)}, bf16[1,4,256,256]{3,2,1,0:T(8,128)(2,1)}, u32[]{:S(2)}) copy-start(bf16[1,4,256,256]{3,2,1,0:T(8,128)(2,1)} %param.13) | copy-start | bytes 1572868
  14.2 146.2 %copy-start.2 = (f32[3]{0:T(128)S(1)}, f32[3]{0:T(128)}, u32[]{:S(2)}) copy-start(f32[3]{0:T(128)} %tau_ref.1) | copy-start | bytes 40
  174.9 0.6 copy-start.1
